TPU v7x, 256 devices: a whole 4x4x8 slice. The times are simulated.
256 devices in a mesh: expert: 128 (over z, x_hi, y, core), replica: 2 (over x_lo).
Axes of the slice: x: 4 (x_hi: 2, x_lo: 2; x = x_hi * 2 + x_lo), y: 4, z: 8, core: 2. Of those that a mesh axis runs over, the one named last changes fastest.
Arguments:
- tokens: bfloat16 [256, 256, 1280], P(('expert', 'replica')), may hold values from -20 to 20
- router: bfloat16 [1280, 128], replicated, may hold values from -0.41926275 to 0.41926275
- w_in: bfloat16 [128, 1280, 2560], P('expert', None, 'replica'), may hold values from -0.15625 to 0.15625
- w_out: bfloat16 [128, 2560, 1280], P('expert', 'replica'), may hold values from -0.125 to 0.125
- cotangent: bfloat16 [256, 256, 1280], P(('expert', 'replica')), may hold values from -6 to 6
Outputs:
- grad_tokens: bfloat16 [256, 256, 1280], P(('expert', 'replica'))
- grad_w_out: bfloat16 [128, 2560, 1280], P('expert', 'replica')
- grad_router: float32 [1280, 128], P('expert')
All inputs are finite; a program needn't handle non-finite values.
Results may differ from a plain program's by a relative error of at most 0.019.
Values may be sent and summed in bfloat16 or wider, within the bound.
A program may use at most 128 MiB of HBM per device.

v0:
```python
import jax
import jax.numpy as jnp
from jax import lax
from jax.sharding import PartitionSpec as P


def gelu_slope(values):
    lower = 0.5 * (1.0 + lax.erf(values * 0.7071067811865476))
    return lower + values * jnp.exp(-0.5 * values * values) * 0.3989422804014327


def body(tokens, router, w_in, w_out, cotangent):
    width = tokens.shape[2]
    logits = jnp.einsum("imd,ds->ims", tokens, router, preferred_element_type=jnp.float32)
    dispatch = jax.nn.softmax(logits, axis=1)
    combine = jax.nn.softmax(logits, axis=2)
    dispatch_low = dispatch.astype(jnp.bfloat16)
    combine_low = combine.astype(jnp.bfloat16)
    slot_in = jnp.einsum(
        "ims,imd->isd", dispatch_low, tokens, preferred_element_type=jnp.float32
    ).astype(jnp.bfloat16)
    arrived = lax.all_to_all(slot_in, "expert", split_axis=1, concat_axis=0, tiled=True)
    slot_rows = arrived.reshape(-1, width)
    own_rows = slot_rows.shape[0]
    first_weight = w_in[0]
    second_weight = w_out[0]
    both_rows = lax.all_gather(slot_rows, "replica", axis=0, tiled=True)
    pre_act = jnp.dot(both_rows, first_weight, preferred_element_type=jnp.float32)
    hidden = jax.nn.gelu(pre_act, approximate=False).astype(jnp.bfloat16)
    picked = hidden
    slot_out = lax.psum_scatter(
        jnp.dot(picked, second_weight, preferred_element_type=jnp.float32).astype(jnp.bfloat16),
        "replica",
        scatter_dimension=0,
        tiled=True,
    )
    returned = lax.all_to_all(
        slot_out.reshape(own_rows, 1, width), "expert", split_axis=0, concat_axis=1, tiled=True
    )
    grad_slot_out = jnp.einsum(
        "ims,imd->isd", combine_low, cotangent, preferred_element_type=jnp.float32
    ).astype(jnp.bfloat16)
    grad_combine = jnp.einsum(
        "imd,isd->ims", cotangent, returned, preferred_element_type=jnp.float32
    )
    grad_arrived = lax.all_to_all(grad_slot_out, "expert", split_axis=1, concat_axis=0, tiled=True)
    grad_rows = grad_arrived.reshape(-1, width)
    both_grads = lax.all_gather(grad_rows, "replica", axis=0, tiled=True)
    grad_hidden = jnp.einsum(
        "rd,fd->rf", both_grads, second_weight, preferred_element_type=jnp.float32
    )
    grad_pre = (grad_hidden * gelu_slope(pre_act)).astype(jnp.bfloat16)
    grad_second = jnp.einsum(
        "rf,rd->fd", hidden, both_grads, preferred_element_type=jnp.float32
    ).astype(jnp.bfloat16)
    picked = grad_pre
    grad_slot_in = lax.psum_scatter(
        jnp.einsum("rf,df->rd", picked, first_weight, preferred_element_type=jnp.float32).astype(
            jnp.bfloat16
        ),
        "replica",
        scatter_dimension=0,
        tiled=True,
    )
    grad_back = lax.all_to_all(
        grad_slot_in.reshape(own_rows, 1, width), "expert", split_axis=0, concat_axis=1, tiled=True
    )
    grad_dispatch = jnp.einsum(
        "imd,isd->ims", tokens, grad_back, preferred_element_type=jnp.float32
    )
    through_dispatch = dispatch * (
        grad_dispatch - jnp.sum(dispatch * grad_dispatch, axis=1, keepdims=True)
    )
    through_combine = combine * (
        grad_combine - jnp.sum(combine * grad_combine, axis=2, keepdims=True)
    )
    grad_logits = (through_dispatch + through_combine).astype(jnp.bfloat16)
    grad_tokens = (
        jnp.einsum("ims,isd->imd", dispatch_low, grad_back, preferred_element_type=jnp.float32)
        + jnp.einsum("ims,ds->imd", grad_logits, router, preferred_element_type=jnp.float32)
    ).astype(jnp.bfloat16)
    router_term = jnp.einsum("imd,ims->ds", tokens, grad_logits, preferred_element_type=jnp.float32)
    paired = lax.psum(router_term.astype(jnp.bfloat16), "replica").astype(jnp.float32)
    grad_router = lax.psum_scatter(paired, "expert", scatter_dimension=0, tiled=True)
    return (grad_tokens, grad_second[None], grad_router)


def solution(mesh):
    placed = (
        P(("expert", "replica"), None, None),
        P(),
        P("expert", None, "replica"),
        P("expert", "replica", None),
        P(("expert", "replica"), None, None),
    )
    return jax.shard_map(
        body,
        mesh=mesh,
        in_specs=placed,
        out_specs=(
            P(("expert", "replica"), None, None),
            P("expert", "replica", None),
            P("expert", None),
        ),
        check_vma=False,
    )
```

profile of v0, /device:TPU:1, one launch (start us, length us, event | category | flops | bytes accessed | tf_op | source)
XLA Modules:
  0.0 863.3 jit_solution(2361048710063872798)
XLA Ops:
  7.2 1.7 fusion.80
  9.1 0.3 fusion.24
  9.4 1.3 copy.49
  10.8 0.5 broadcast.45
  11.3 4.3 reduce.12
  15.5 1.8 reshape.132
  17.3 16.8 %all-to-all-start.1 = ((bf16[128,2,640]{2,1,0:T(2,128)(2,1)}), bf16[128,2,640]{2,1,0:T(2,128)(2,1)}, u32[]{:S(2)}, u32[]{:S(2)}) async-start(bf16[128,2,640]{2,1,0:T(2,128)(2,1)} %reshape.132), calls=%async_computation.1 | async-start | bytes 655360 | tf_op jit(solution)/shard_map/all_to_all | solution.py:22
  34.1 1.5 fusion.23
  35.6 1.3 copy.50
  37.0 4.3 reduce.13
  41.2 1.8 reshape.136
  43.0 8.1 all-to-all-done.1
  51.1 6.3 all-to-all-start
  57.4 3.2 reshape.133
  60.7 1.1 copy.21
  61.8 10.7 %all-gather.1 = bf16[1,256,1280]{2,1,0:T(8,128)(2,1)S(1)} all-gather(bf16[1,128,1280]{2,1,0:T(8,128)(2,1)S(1)} %copy.21), channel_id=3, replica_groups=mesh['expert'=128,'replica'=2] {'replica'}, dimensions={1}, use_global_device_ids=true | all-gather | bytes 983040 | tf_op jit(solution)/shard_map/all_gather | solution.py:27
  72.5 4.6 fusion.32
  77.1 0.8 copy-done.7
  77.9 1.9 fusion.13
  79.9 3.2 reshape.137
  83.1 1.1 copy.19
  84.2 8.9 %all-gather = bf16[1,256,1280]{2,1,0:T(8,128)(2,1)} all-gather(bf16[1,128,1280]{2,1,0:T(8,128)(2,1)S(1)} %copy.19), channel_id=2, replica_groups=mesh['expert'=128,'replica'=2] {'replica'}, dimensions={1}, use_global_device_ids=true | all-gather | bytes 983040 | tf_op jit(solution)/shard_map/all_gather | solution.py:48
  93.1 5.4 fusion.16
  98.5 4.1 reduce-scatter.6.cloned.1.call-done
  102.6 2.5 reduce.15
  105.1 1.8 reshape.134
  106.9 13.5 %all-to-all-start.3 = ((bf16[128,2,640]{2,1,0:T(2,128)(2,1)}), bf16[128,2,640]{2,1,0:T(2,128)(2,1)}, u32[]{:S(2)}, u32[]{:S(2)}) async-start(bf16[128,2,640]{2,1,0:T(2,128)(2,1)} %reshape.134), calls=%async_computation.5 | async-start | bytes 655360 | tf_op jit(solution)/shard_map/all_to_all | solution.py:37
  120.5 10.1 %reduce-scatter.4.cloned.1.call-done = bf16[128,1280]{1,0:T(8,128)(2,1)} async-done(((bf16[256,1280]{1,0:T(8,128)(2,1)}), bf16[128,1280]{1,0:T(8,128)(2,1)}) %reduce-scatter.4.cloned.1.call-update) | async-done | bytes 327696 | tf_op jit(solution)/shard_map/reduce_scatter | solution.py:57
  130.5 2.5 reduce.14
  133.0 1.8 reshape.138
  134.8 2.6 all-to-all-done.3
  137.4 11.7 %all-to-all-start.2 = ((bf16[128,2,640]{2,1,0:T(2,128)(2,1)}), bf16[128,2,640]{2,1,0:T(2,128)(2,1)}, u32[]{:S(2)}, u32[]{:S(2)}) async-start(bf16[128,2,640]{2,1,0:T(2,128)(2,1)} %reshape.138), calls=%async_computation.3 | async-start | bytes 655360 | tf_op jit(solution)/shard_map/all_to_all | solution.py:65
  149.1 0.3 all-reduce.4.cloned.1.call-start
  149.4 0.6 dynamic-slice
  150.6 4.1 fusion
  154.7 3.2 reshape.135
  157.9 1.6 convolution_bitcast_fusion
  159.6 6.5 all-to-all-done.2
  166.1 3.2 reshape.139
  169.3 1.7 multiply_reduce_fusion.1
  171.0 1.1 add_convert_fusion
  172.1 1.0 fusion.25
  173.1 1.5 fusion.61
  174.6 1.2 fusion.22
  175.7 28.2 %all-reduce.4.cloned.1.call-done = bf16[1280,128]{0,1:T(8,128)(2,1)} async-done(((bf16[1280,128]{0,1:T(8,128)(2,1)}), bf16[1280,128]{0,1:T(8,128)(2,1)}) %all-reduce.4.cloned.1.call-update) | async-done | bytes 327696 | tf_op jit(solution)/shard_map/psum | solution.py:83
  203.9 651.1 %all-reduce.5 = f32[1280,128]{0,1:T(8,128)} all-reduce(bf16[1280,128]{0,1:T(8,128)(2,1)} %all-reduce.4.cloned.1.call-done), channel_id=6, replica_groups=mesh['expert'=128,'replica'=2] {'expert'}, use_global_device_ids=true, to_apply=%region_9.0.clone | all-reduce | flops 163840 | bytes 983040
  855.1 1.0 constant_dynamic-slice_fusion
  856.0 0.7 copy.26
  (22 shorter events, 0.4 us)
Async XLA Ops:
  7.2 65.3 %copy-start = (bf16[1,1280,1280]{2,1,0:T(8,128)(2,1)S(1)}, bf16[1,1280,1280]{2,1,0:T(8,128)(2,1)}, u32[]{:S(2)}) copy-start(bf16[1,1280,1280]{2,1,0:T(8,128)(2,1)} %param.7) | copy-start | bytes 9830404
  7.2 1.9 copy-start.1
  17.3 33.7 %all-to-all-start.1 = ((bf16[128,2,640]{2,1,0:T(2,128)(2,1)}), bf16[128,2,640]{2,1,0:T(2,128)(2,1)}, u32[]{:S(2)}, u32[]{:S(2)}) async-start(bf16[128,2,640]{2,1,0:T(2,128)(2,1)} %reshape.132), calls=%async_computation.1 | async-start | bytes 655360 | tf_op jit(solution)/shard_map/all_to_all | solution.py:22
  51.1 28.8 %all-to-all-start = ((bf16[128,2,640]{2,1,0:T(2,128)(2,1)}), bf16[128,2,640]{2,1,0:T(2,128)(2,1)}, u32[]{:S(2)}, u32[]{:S(2)}) async-start(bf16[128,2,640]{2,1,0:T(2,128)(2,1)} %reshape.136), calls=%async_computation | async-start | bytes 655360 | tf_op jit(solution)/shard_map/all_to_all | solution.py:46
  57.4 45.2 %reduce-scatter.6.cloned.1.call-start = ((), (), s32[]{:S(2)}) async-start(), calls=%async_computation.7 | async-start | bytes 983040 | tf_op jit(solution)/shard_map/reduce_scatter | solution.py:31
  72.5 5.4 copy-start.5
  77.1 0.8 copy-start.7
  79.8 50.7 %reduce-scatter.4.cloned.1.call-start = ((), (), s32[]{:S(2)}) async-start(), calls=%async_computation.6 | async-start | bytes 983040 | tf_op jit(solution)/shard_map/reduce_scatter | solution.py:57
  106.9 42.5 %copy-start.6 = (u32[256]{0:T(256)S(1)}, u32[256]{0:T(256)}, u32[]{:S(2)}) copy-start(u32[256]{0:T(256)} %constant.75) | copy-start | bytes 3076
  106.9 30.5 %all-to-all-start.3 = ((bf16[128,2,640]{2,1,0:T(2,128)(2,1)}), bf16[128,2,640]{2,1,0:T(2,128)(2,1)}, u32[]{:S(2)}, u32[]{:S(2)}) async-start(bf16[128,2,640]{2,1,0:T(2,128)(2,1)} %reshape.134), calls=%async_computation.5 | async-start | bytes 655360 | tf_op jit(solution)/shard_map/all_to_all | solution.py:37
  137.4 28.7 %all-to-all-start.2 = ((bf16[128,2,640]{2,1,0:T(2,128)(2,1)}), bf16[128,2,640]{2,1,0:T(2,128)(2,1)}, u32[]{:S(2)}, u32[]{:S(2)}) async-start(bf16[128,2,640]{2,1,0:T(2,128)(2,1)} %reshape.138), calls=%async_computation.3 | async-start | bytes 655360 | tf_op jit(solution)/shard_map/all_to_all | solution.py:65
  149.1 54.8 %all-reduce.4.cloned.1.call-start = ((), (), s32[]{:S(2)}) async-start(), calls=%async_computation.8 | async-start | bytes 655360 | tf_op jit(solution)/shard_map/psum | solution.py:83
  159.5 11.4 %copy-start.4 = (f32[256,128]{1,0:T(8,128)}, f32[256,128]{1,0:T(8,128)S(1)}, u32[]{:S(2)}) copy-start(f32[256,128]{1,0:T(8,128)S(1)} %convolution_bitcast_fusion) | copy-start | bytes 393220
  169.3 2.8 copy-start.2
  173.1 1.5 copy-start.3
Sparse Core Ops, SparseCore 0:
  80.0 22.6 reduce-scatter.5
  105.9 24.5 reduce-scatter.3
  173.2 30.6 all-reduce.3
where the time goes:
time: 870 us; the launch traced here: 863 us
  blocking collectives  671 us (77%)
  waiting for transfers between devices  59.6 us (7%)
  starting transfers between devices  48.7 us (6%)
  local copies, waits for them, and re-layouts  28.5 us (3%)
  matrix products  26.4 us (3%)
  other arithmetic  14.8 us (2%)
  between operations  14.6 us (2%)
    unnamed x1, blocking collectives  651 us
    psum x1, waiting for transfers between devices, body(): lax.psum(router_term.astype(jnp.bfloat16), 'replica').astype(jnp.float32)  28.2 us
    unnamed x28, local copies, waits for them, and re-layouts  23.6 us
  transfers between devices with their start and end apart: 7, of which 6 were waited for; matrix products, arithmetic and copies ran while one was open for 6% of the time, Pallas kernels for 0%

commit v1 on v0

--- a/solution.py
+++ b/solution.py
@@ -80,8 +80,12 @@
         + jnp.einsum("ims,ds->imd", grad_logits, router, preferred_element_type=jnp.float32)
     ).astype(jnp.bfloat16)
     router_term = jnp.einsum("imd,ims->ds", tokens, grad_logits, preferred_element_type=jnp.float32)
-    paired = lax.psum(router_term.astype(jnp.bfloat16), "replica").astype(jnp.float32)
-    grad_router = lax.psum_scatter(paired, "expert", scatter_dimension=0, tiled=True)
+    shares = lax.all_to_all(
+        router_term.astype(jnp.bfloat16).reshape(128, -1, router_term.shape[1]),
+        "expert", split_axis=0, concat_axis=0, tiled=True,
+    )
+    group_sum = jnp.sum(shares.astype(jnp.float32), axis=0)
+    grad_router = lax.psum(group_sum, "replica")
     return (grad_tokens, grad_second[None], grad_router)
 
 

time: 870 us -> 217 us (0.25)
  blocking collectives: 671 us -> 24 us
  waiting for transfers between devices: 59.6 us -> 50.8 us
    unnamed x1 -> x0, blocking collectives: 651 us -> none
    psum x1 -> x0, waiting for transfers between devices: 28.2 us -> none  [body(): lax.psum(router_term.astype(jnp.bfloat16), 'replica').astype(jnp.float32)]
    all_to_all x0 -> x1, waiting for transfers between devices: none -> 13.9 us  [body(): lax.all_to_all(router_term.astype(jnp.bfloat16).reshape(128, -1, router_t...]
    unnamed x28 -> x25, local copies, waits for them, and re-layouts: 23.6 us -> 22 us
  transfers between devices with their start and end apart: 7 -> 7, of which waited for: 6 -> 6; matrix products, arithmetic and copies ran while one was open for 6% -> 22% of each run, Pallas kernels for 0% -> 0%
where the time goes in v1:
time: 217 us; the launch traced here: 216 us
  starting transfers between devices  55 us (25%)
  waiting for transfers between devices  50.8 us (23%)
  local copies, waits for them, and re-layouts  30.7 us (14%)
  matrix products  25.3 us (12%)
  blocking collectives  24 us (11%)
  other arithmetic  15.9 us (7%)
  between operations  14.2 us (7%)
    unnamed x25, local copies, waits for them, and re-layouts  22 us
    all_to_all x1, starting transfers between devices, body(): lax.all_to_all(slot_in, 'expert', split_axis=1, concat_axis=0, tiled=True)  16.8 us
    all_to_all x1, waiting for transfers between devices, body(): lax.all_to_all(router_term.astype(jnp.bfloat16).reshape(128, -1, router_t...  13.9 us
    all_to_all x1, starting transfers between devices, body(): lax.all_to_all(slot_out.reshape(own_rows, 1, width), 'expert', split_axis...  13.4 us
    all_to_all x1, waiting for transfers between devices, body(): lax.all_to_all(grad_slot_in.reshape(own_rows, 1, width), 'expert', split_...  12.1 us
    all_to_all x1, starting transfers between devices, body(): lax.all_to_all(grad_slot_in.reshape(own_rows, 1, width), 'expert', split_...  11.9 us
    all_gather x1, blocking collectives, body(): both_rows = lax.all_gather(slot_rows, 'replica', axis=0, tiled=True)  10.7 us
    reduce_scatter x1, waiting for transfers between devices, body(): lax.psum_scatter(jnp.einsum('rf,df->rd', picked, first_weight, preferred_...  10.2 us
  transfers between devices with their start and end apart: 7, of which 6 were waited for; matrix products, arithmetic and copies ran while one was open for 22% of the time, Pallas kernels for 0%

profile of v1, /device:TPU:1, one launch (start us, length us, event | category | flops | bytes accessed | tf_op | source)
XLA Modules:
  0.0 215.9 jit_solution(4684188381099875958)
XLA Ops:
  7.2 1.7 fusion.80
  9.4 1.3 copy.49
  10.8 0.5 broadcast.45
  11.3 4.3 %reduce.12 = bf16[128,1280]{1,0:T(8,128)(2,1)} reduce(bf16[128,1,1280]{2,1,0:T(2,128)(2,1)} %bitcast.91, bf16[]{:T(256)} %broadcast.45), dimensions={1}, to_apply=%bitcast.89.reduce_sub_computation | reduce | bytes 655362
  15.5 1.8 reshape.133
  17.3 16.8 %all-to-all-start.1 = ((bf16[128,2,640]{2,1,0:T(2,128)(2,1)}), bf16[128,2,640]{2,1,0:T(2,128)(2,1)}, u32[]{:S(2)}, u32[]{:S(2)}) async-start(bf16[128,2,640]{2,1,0:T(2,128)(2,1)} %reshape.133), calls=%async_computation.1 | async-start | bytes 655360 | tf_op jit(solution)/shard_map/all_to_all | solution.py:22
  34.1 1.5 fusion.23
  35.6 1.3 copy.50
  37.0 4.3 %reduce.13 = bf16[128,1280]{1,0:T(8,128)(2,1)} reduce(bf16[128,1,1280]{2,1,0:T(2,128)(2,1)} %bitcast.92, bf16[]{:T(256)} %broadcast.45), dimensions={1}, to_apply=%bitcast.90.reduce_sub_computation | reduce | bytes 655362
  41.2 1.8 reshape.135
  43.0 8.1 %all-to-all-done.1 = bf16[128,2,640]{2,1,0:T(2,128)(2,1)} async-done(((bf16[128,2,640]{2,1,0:T(2,128)(2,1)}), bf16[128,2,640]{2,1,0:T(2,128)(2,1)}, u32[]{:S(2)}, u32[]{:S(2)}) %all-to-all-start.1) | async-done | bytes 327712 | tf_op jit(solution)/shard_map/all_to_all | solution.py:22
  51.1 6.3 %all-to-all-start = ((bf16[128,2,640]{2,1,0:T(2,128)(2,1)}), bf16[128,2,640]{2,1,0:T(2,128)(2,1)}, u32[]{:S(2)}, u32[]{:S(2)}) async-start(bf16[128,2,640]{2,1,0:T(2,128)(2,1)} %reshape.135), calls=%async_computation | async-start | bytes 655360 | tf_op jit(solution)/shard_map/all_to_all | solution.py:46
  57.4 3.2 %reshape.134 = bf16[128,1,1280]{2,1,0:T(2,128)(2,1)} reshape(bf16[128,2,640]{2,1,0:T(2,128)(2,1)} %all-to-all-done.1) | data formatting | bytes 655360
  60.7 1.1 copy.23
  61.8 10.7 %all-gather.1 = bf16[1,256,1280]{2,1,0:T(8,128)(2,1)S(1)} all-gather(bf16[1,128,1280]{2,1,0:T(8,128)(2,1)S(1)} %copy.23), channel_id=3, replica_groups=mesh['expert'=128,'replica'=2] {'replica'}, dimensions={1}, use_global_device_ids=true | all-gather | bytes 983040 | tf_op jit(solution)/shard_map/all_gather | solution.py:27
  72.5 4.6 %fusion.32 = (bf16[256,1280]{1,0:T(8,128)(2,1)S(1)}, f32[256,1280]{1,0:T(8,128)}) fusion(bf16[1,1280,1280]{2,1,0:T(8,128)(2,1)S(1)} %copy-done, bf16[1,256,1280]{2,1,0:T(8,128)(2,1)S(1)} %all-gather.1), kind=kOutput, calls=%fused_computation.31 | convolution fusion | flops 860160000 | bytes 5898240 | tf_op jit(solution)/shard_map/dot_general | solution.py:28
  77.1 0.8 copy-done.7
  77.9 1.9 fusion.13
  79.9 3.2 %reshape.136 = bf16[128,1,1280]{2,1,0:T(2,128)(2,1)} reshape(bf16[128,2,640]{2,1,0:T(2,128)(2,1)} %all-to-all-done) | data formatting | bytes 655360
  83.1 1.1 copy.21
  84.2 8.9 %all-gather = bf16[1,256,1280]{2,1,0:T(8,128)(2,1)} all-gather(bf16[1,128,1280]{2,1,0:T(8,128)(2,1)S(1)} %copy.21), channel_id=2, replica_groups=mesh['expert'=128,'replica'=2] {'replica'}, dimensions={1}, use_global_device_ids=true | all-gather | bytes 983040 | tf_op jit(solution)/shard_map/all_gather | solution.py:48
  93.1 5.4 %fusion.16 = bf16[256,1280]{1,0:T(8,128)(2,1)} fusion(bf16[1,1280,1280]{2,1,0:T(8,128)(2,1)S(1)} %copy-done, bf16[1,1280,1280]{2,1,0:T(8,128)(2,1)} %param.8, f32[256,1280]{1,0:T(8,128)} %get-tuple-element.11, bf16[1,256,1280]{2,1,0:T(8,128)(2,1)} %all-gather), kind=kOutput, calls=%fused_computation.14 | convolution fusion | flops 1681326080 | bytes 9175040 | tf_op jit(solution)/shard_map/rf,df->rd/dot_general | solution.py:58
  98.5 4.1 %reduce-scatter.5.cloned.1.call-done = bf16[128,1280]{1,0:T(8,128)(2,1)} async-done(((bf16[256,1280]{1,0:T(8,128)(2,1)}), bf16[128,1280]{1,0:T(8,128)(2,1)}) %reduce-scatter.5.cloned.1.call-update) | async-done | bytes 327696 | tf_op jit(solution)/shard_map/reduce_scatter | solution.py:31
  102.6 2.5 %reduce.15 = bf16[128,1280]{1,0:T(8,128)(2,1)} reduce(bf16[128,1,1280]{2,0,1:T(8,128)(2,1)} %bitcast.95, bf16[]{:T(256)} %broadcast.45), dimensions={1}, to_apply=%copy.26.reduce_sub_computation | reduce | bytes 655362 | tf_op jit(solution)/shard_map/reshape | solution.py:38
  105.1 1.8 reshape.139
  106.9 13.4 %all-to-all-start.3 = ((bf16[128,2,640]{2,1,0:T(2,128)(2,1)}), bf16[128,2,640]{2,1,0:T(2,128)(2,1)}, u32[]{:S(2)}, u32[]{:S(2)}) async-start(bf16[128,2,640]{2,1,0:T(2,128)(2,1)} %reshape.139), calls=%async_computation.5 | async-start | bytes 655360 | tf_op jit(solution)/shard_map/all_to_all | solution.py:37
  120.3 10.2 %reduce-scatter.3.cloned.1.call-done = bf16[128,1280]{1,0:T(8,128)(2,1)} async-done(((bf16[256,1280]{1,0:T(8,128)(2,1)}), bf16[128,1280]{1,0:T(8,128)(2,1)}) %reduce-scatter.3.cloned.1.call-update) | async-done | bytes 327696 | tf_op jit(solution)/shard_map/reduce_scatter | solution.py:57
  130.5 2.5 %reduce.14 = bf16[128,1280]{1,0:T(8,128)(2,1)} reduce(bf16[128,1,1280]{2,0,1:T(8,128)(2,1)} %bitcast.96, bf16[]{:T(256)} %broadcast.45), dimensions={1}, to_apply=%copy.24.reduce_sub_computation | reduce | bytes 655362 | tf_op jit(solution)/shard_map/reshape | solution.py:66
  133.0 1.8 reshape.137
  134.8 2.5 %all-to-all-done.3 = bf16[128,2,640]{2,1,0:T(2,128)(2,1)} async-done(((bf16[128,2,640]{2,1,0:T(2,128)(2,1)}), bf16[128,2,640]{2,1,0:T(2,128)(2,1)}, u32[]{:S(2)}, u32[]{:S(2)}) %all-to-all-start.3) | async-done | bytes 327712 | tf_op jit(solution)/shard_map/all_to_all | solution.py:37
  137.2 11.9 %all-to-all-start.2 = ((bf16[128,2,640]{2,1,0:T(2,128)(2,1)}), bf16[128,2,640]{2,1,0:T(2,128)(2,1)}, u32[]{:S(2)}, u32[]{:S(2)}) async-start(bf16[128,2,640]{2,1,0:T(2,128)(2,1)} %reshape.137), calls=%async_computation.3 | async-start | bytes 655360 | tf_op jit(solution)/shard_map/all_to_all | solution.py:65
  149.1 3.2 %reshape.140 = bf16[128,1,1280]{2,1,0:T(2,128)(2,1)} reshape(bf16[128,2,640]{2,1,0:T(2,128)(2,1)} %all-to-all-done.3) | data formatting | bytes 655360
  152.4 1.6 convolution_bitcast_fusion
  154.0 12.1 %all-to-all-done.2 = bf16[128,2,640]{2,1,0:T(2,128)(2,1)} async-done(((bf16[128,2,640]{2,1,0:T(2,128)(2,1)}), bf16[128,2,640]{2,1,0:T(2,128)(2,1)}, u32[]{:S(2)}, u32[]{:S(2)}) %all-to-all-start.2) | async-done | bytes 327712 | tf_op jit(solution)/shard_map/all_to_all | solution.py:65
  166.1 3.2 %reshape.138 = bf16[128,1,1280]{2,1,0:T(2,128)(2,1)} reshape(bf16[128,2,640]{2,1,0:T(2,128)(2,1)} %all-to-all-done.2) | data formatting | bytes 655360
  169.3 1.7 multiply_reduce_fusion.1
  171.0 1.1 add_convert_fusion
  172.1 1.0 fusion.25
  173.1 1.9 copy.28
  175.0 1.9 reshape.130
  176.9 6.4 %all-to-all-start.4 = ((bf16[128,10,128]{2,1,0:T(8,128)(2,1)}), bf16[128,10,128]{2,1,0:T(8,128)(2,1)}, u32[]{:S(2)}, u32[]{:S(2)}) async-start(bf16[128,10,128]{2,1,0:T(8,128)(2,1)} %reshape.130), calls=%async_computation.6 | async-start | bytes 1048576 | tf_op jit(solution)/shard_map/all_to_all | solution.py:83
  183.3 4.1 %fusion = bf16[1,1280,1280]{2,1,0:T(8,128)(2,1)} fusion(bf16[256,1280]{1,0:T(8,128)(2,1)} %copy-done.7, bf16[1,256,1280]{2,1,0:T(8,128)(2,1)} %all-gather), kind=kOutput, calls=%fused_computation.1 | convolution fusion | flops 840499200 | bytes 4587520 | tf_op jit(solution)/shard_map/rf,rd->fd/dot_general | solution.py:53
  187.4 0.3 fusion.61
  187.8 0.7 copy-done.4
  188.4 1.2 fusion.22
  189.6 13.9 %all-to-all-done.4 = bf16[128,10,128]{2,1,0:T(8,128)(2,1)} async-done(((bf16[128,10,128]{2,1,0:T(8,128)(2,1)}), bf16[128,10,128]{2,1,0:T(8,128)(2,1)}, u32[]{:S(2)}, u32[]{:S(2)}) %all-to-all-start.4) | async-done | bytes 327712 | tf_op jit(solution)/shard_map/all_to_all | solution.py:83
  203.5 1.2 convert_reduce_fusion
  204.6 4.4 %psum.7 = f32[10,128]{1,0:T(8,128)} all-reduce(f32[10,128]{1,0:T(8,128)S(1)} %convert_reduce_fusion), channel_id=1, replica_groups=mesh['expert'=128,'replica'=2] {'replica'}, use_global_device_ids=true, to_apply=%region_9.0 | all-reduce | flops 1280 | bytes 10240 | tf_op jit(solution)/shard_map/psum | solution.py:88
  (21 shorter events, 0.6 us)
Async XLA Ops:
  7.2 65.3 %copy-start = (bf16[1,1280,1280]{2,1,0:T(8,128)(2,1)S(1)}, bf16[1,1280,1280]{2,1,0:T(8,128)(2,1)}, u32[]{:S(2)}) copy-start(bf16[1,1280,1280]{2,1,0:T(8,128)(2,1)} %param.7) | copy-start | bytes 9830404
  7.2 1.9 copy-start.1
  17.3 33.7 %all-to-all-start.1 = ((bf16[128,2,640]{2,1,0:T(2,128)(2,1)}), bf16[128,2,640]{2,1,0:T(2,128)(2,1)}, u32[]{:S(2)}, u32[]{:S(2)}) async-start(bf16[128,2,640]{2,1,0:T(2,128)(2,1)} %reshape.133), calls=%async_computation.1 | async-start | bytes 655360 | tf_op jit(solution)/shard_map/all_to_all | solution.py:22
  51.1 28.8 %all-to-all-start = ((bf16[128,2,640]{2,1,0:T(2,128)(2,1)}), bf16[128,2,640]{2,1,0:T(2,128)(2,1)}, u32[]{:S(2)}, u32[]{:S(2)}) async-start(bf16[128,2,640]{2,1,0:T(2,128)(2,1)} %reshape.135), calls=%async_computation | async-start | bytes 655360 | tf_op jit(solution)/shard_map/all_to_all | solution.py:46
  57.4 45.2 %reduce-scatter.5.cloned.1.call-start = ((), (), s32[]{:S(2)}) async-start(), calls=%async_computation.8 | async-start | bytes 983040 | tf_op jit(solution)/shard_map/reduce_scatter | solution.py:31
  72.5 5.4 %copy-start.6 = (bf16[1,1280,1280]{2,1,0:T(8,128)(2,1)S(1)}, bf16[1,1280,1280]{2,1,0:T(8,128)(2,1)}, u32[]{:S(2)}) copy-start(bf16[1,1280,1280]{2,1,0:T(8,128)(2,1)} %param.8) | copy-start | bytes 9830404
  77.1 0.8 copy-start.7
  79.8 50.7 %reduce-scatter.3.cloned.1.call-start = ((), (), s32[]{:S(2)}) async-start(), calls=%async_computation.7 | async-start | bytes 983040 | tf_op jit(solution)/shard_map/reduce_scatter | solution.py:57
  106.9 30.3 %all-to-all-start.3 = ((bf16[128,2,640]{2,1,0:T(2,128)(2,1)}), bf16[128,2,640]{2,1,0:T(2,128)(2,1)}, u32[]{:S(2)}, u32[]{:S(2)}) async-start(bf16[128,2,640]{2,1,0:T(2,128)(2,1)} %reshape.139), calls=%async_computation.5 | async-start | bytes 655360 | tf_op jit(solution)/shard_map/all_to_all | solution.py:37
  137.2 28.8 %all-to-all-start.2 = ((bf16[128,2,640]{2,1,0:T(2,128)(2,1)}), bf16[128,2,640]{2,1,0:T(2,128)(2,1)}, u32[]{:S(2)}, u32[]{:S(2)}) async-start(bf16[128,2,640]{2,1,0:T(2,128)(2,1)} %reshape.137), calls=%async_computation.3 | async-start | bytes 655360 | tf_op jit(solution)/shard_map/all_to_all | solution.py:65
  154.0 17.0 %copy-start.5 = (f32[256,128]{1,0:T(8,128)}, f32[256,128]{1,0:T(8,128)S(1)}, u32[]{:S(2)}) copy-start(f32[256,128]{1,0:T(8,128)S(1)} %convolution_bitcast_fusion) | copy-start | bytes 393220
  169.3 2.8 %copy-start.2 = (bf16[1,256,1280]{2,1,0:T(8,128)(2,1)S(1)}, bf16[1,256,1280]{2,1,0:T(8,128)(2,1)}, u32[]{:S(2)}) copy-start(bf16[1,256,1280]{2,1,0:T(8,128)(2,1)} %param.5) | copy-start | bytes 1966084
  176.9 26.6 %all-to-all-start.4 = ((bf16[128,10,128]{2,1,0:T(8,128)(2,1)}), bf16[128,10,128]{2,1,0:T(8,128)(2,1)}, u32[]{:S(2)}, u32[]{:S(2)}) async-start(bf16[128,10,128]{2,1,0:T(8,128)(2,1)} %reshape.130), calls=%async_computation.6 | async-start | bytes 1048576 | tf_op jit(solution)/shard_map/all_to_all | solution.py:83
  183.3 4.1 %copy-start.3 = (bf16[128,1,1280]{2,1,0:T(2,128)(2,1)S(1)}, bf16[128,1,1280]{2,1,0:T(2,128)(2,1)}, u32[]{:S(2)}) copy-start(bf16[128,1,1280]{2,1,0:T(2,128)(2,1)} %reshape.138) | copy-start | bytes 983044
  187.4 1.0 copy-start.4
Sparse Core Ops, SparseCore 0:
  80.0 22.6 reduce-scatter.4
  105.9 24.5 reduce-scatter.2

commit v2 on v0

v2 whole, which is shorter than its diff:
```python
import functools

import jax
import jax.numpy as jnp
from jax import lax
from jax.experimental import pallas as pl
from jax.experimental.pallas import tpu as pltpu
from jax.sharding import PartitionSpec as P

F32 = jnp.float32
BF16 = jnp.bfloat16
MESH = pl.DeviceIdType.MESH
PLANE = 16


def tile_of(width):
    return 256 if width % 256 == 0 else width


def matmul(a, b):
    return jnp.dot(a, b, preferred_element_type=F32)


def matmul_nt(a, b):
    return lax.dot_general(a, b, (((1,), (1,)), ((), ())), preferred_element_type=F32)


def matmul_tn(a, b):
    return lax.dot_general(a, b, (((0,), (0,)), ((), ())), preferred_element_type=F32)


def softmax(logits, axis):
    raised = jnp.exp(logits - jnp.max(logits, axis=axis, keepdims=True))
    return raised / jnp.sum(raised, axis=axis, keepdims=True)


def kernel(
    nz, np_, share, pad,
    tok_hbm, rt_hbm, win_hbm, wout_hbm, cot_hbm,
    gt_hbm, gw_hbm, gr_ref,
    tok, rt, win, wout, cot, tok_t,
    disp, comb, through,
    slots, gathered, bundles, arrived, rows,
    hid, slope, gpre, wide, partial, partials, sent_back, returned,
    rsend, rmid, rpad, rall, gw, gt,
    load_sem, store_sem, zs_sem, zr_sem, ps_sem, pr_sem,
):
    e = lax.axis_index("expert")
    r = lax.axis_index("replica")
    z = lax.div(e, np_)
    p = lax.rem(e, np_)
    nq = 2 * np_
    q = r * np_ + p
    experts = nz * np_
    width = tok.shape[1]
    half = width // 2
    inner = hid.shape[1]

    def z_peer(k):
        other = lax.rem(z + k, nz)
        return other, (other * np_ + p, r)

    def z_source(k):
        return lax.rem(z + nz - k, nz)

    def plane_peer(k):
        other = lax.rem(q + k, nq)
        return other, (z * np_ + lax.rem(other, np_), lax.div(other, np_))

    def plane_source(k):
        return lax.rem(q + nq - k, nq)

    barrier = pltpu.get_barrier_semaphore()

    @pl.loop(1, nz)
    def _(k):
        pl.semaphore_signal(barrier, inc=1, device_id=z_peer(k)[1], device_id_type=MESH)

    @pl.loop(1, nq)
    def _(k):
        pl.semaphore_signal(barrier, inc=1, device_id=plane_peer(k)[1], device_id_type=MESH)

    loads = [
        pltpu.make_async_copy(src, dst, load_sem.at[i])
        for i, (src, dst) in enumerate(
            ((tok_hbm, tok), (rt_hbm, rt), (cot_hbm, cot), (win_hbm, win), (wout_hbm, wout)))
    ]
    for load in loads:
        load.start()

    def z_copy(i, src, dst, k, at):
        other, device = z_peer(k)
        return pltpu.make_async_remote_copy(
            src_ref=src.at[other], dst_ref=dst.at[at], send_sem=zs_sem.at[i, k],
            recv_sem=zr_sem.at[i, k], device_id=device, device_id_type=MESH)

    def z_send(i, src, dst):
        @pl.loop(1, nz)
        def _(k):
            z_copy(i, src, dst, k, z).start()
        dst[z] = src[z]

    def z_wait(i, src, dst):
        @pl.loop(1, nz)
        def _(k):
            z_copy(i, src, dst, k, z_source(k)).wait_recv()

    def z_drain(i, src, dst):
        @pl.loop(1, nz)
        def _(k):
            z_copy(i, src, dst, k, z).wait_send()

    def plane_copy(i, src, dst, k, at, fold):
        other, device = plane_peer(k)
        return pltpu.make_async_remote_copy(
            src_ref=src.at[lax.rem(other, np_) if fold else other], dst_ref=dst.at[at],
            send_sem=ps_sem.at[i, k], recv_sem=pr_sem.at[i, k],
            device_id=device, device_id_type=MESH)

    def plane_send(i, src, dst, fold):
        @pl.loop(1, nq)
        def _(k):
            plane_copy(i, src, dst, k, q, fold).start()
        dst[q] = src[p if fold else q]

    def plane_wait(i, src, dst, fold):
        @pl.loop(1, nq)
        def _(k):
            plane_copy(i, src, dst, k, plane_source(k), fold).wait_recv()

    def plane_drain(i, src, dst, fold):
        @pl.loop(1, nq)
        def _(k):
            plane_copy(i, src, dst, k, q, fold).wait_send()

    loads[0].wait()
    loads[1].wait()
    logits = matmul(tok[...], rt[...])
    dispatch = softmax(logits, 0)
    disp[...] = dispatch
    slots[0] = matmul(dispatch.T.astype(BF16), tok[...]).astype(BF16).reshape(nz, np_, width)
    pl.semaphore_wait(barrier, nz - 1 + nq - 1)
    z_send(0, slots.at[0], gathered.at[0])
    combine = softmax(logits, 1)
    comb[...] = combine
    loads[2].wait()
    slots[1] = matmul(combine.T.astype(BF16), cot[...]).astype(BF16).reshape(nz, np_, width)
    z_send(1, slots.at[1], gathered.at[1])
    tok_t[...] = tok[...].T

    span = 2 * nz
    at_row = lax.broadcasted_iota(jnp.int32, (np_ * span, experts), 0)
    at_col = lax.broadcasted_iota(jnp.int32, (np_ * span, experts), 1)
    spread = [
        jnp.where(
            at_row == lax.rem(at_col, np_) * span + h * nz + lax.div(at_col, np_), 1.0, 0.0
        ).astype(BF16)
        for h in range(2)
    ]
    for i in range(2):
        z_wait(i, slots.at[i], gathered.at[i])
        block = gathered[i].reshape(experts, width)
        bundles[i] = (
            matmul(spread[0], block[:, :half]) + matmul(spread[1], block[:, half:])
        ).astype(BF16).reshape(np_, span, half)
        plane_send(2 * i, bundles.at[i], arrived.at[i], True)

    def unbundle(i):
        plane_wait(2 * i, bundles.at[i], arrived.at[i], True)
        block = arrived[i].astype(F32)
        for h in range(2):
            rows[i, :, h * half:(h + 1) * half] = (
                block[:, h * nz:(h + 1) * nz, :].reshape(nq * nz, half).astype(BF16))

    def bundle(i):
        partial[i] = wide[...].astype(BF16)
        plane_send(2 * i + 1, partial.at[i], partials.at[i], False)

    step = tile_of(inner)
    unbundle(0)
    loads[3].wait()

    @pl.loop(0, inner // step)
    def _(t):
        at = pl.ds(pl.multiple_of(t * step, step), step)
        pre = matmul(rows[0], win[:, at])
        lower = 0.5 * (1.0 + lax.erf(pre * 0.7071067811865476))
        hid[:, at] = (pre * lower).astype(BF16)
        slope[:, at] = lower + pre * jnp.exp(-0.5 * pre * pre) * 0.3989422804014327

    loads[4].wait()
    for h in range(2):
        wide[:, h * nz:(h + 1) * nz, :] = matmul(
            hid[...], wout[:, h * half:(h + 1) * half]).reshape(nq, nz, half)
    bundle(0)

    unbundle(1)

    @pl.loop(0, inner // step)
    def _(t):
        at = pl.ds(pl.multiple_of(t * step, step), step)
        gpre[:, at] = (matmul_nt(rows[1], wout[at, :]) * slope[:, at]).astype(BF16)

    for h in range(2):
        wide[:, h * nz:(h + 1) * nz, :] = matmul_nt(
            gpre[...], win[h * half:(h + 1) * half, :]).reshape(nq, nz, half)
    bundle(1)

    def gateway_back(i):
        plane_wait(2 * i + 1, partial.at[i], partials.at[i], False)
        both = (partials[i, :np_].astype(F32) + partials[i, np_:].astype(F32)).astype(BF16)
        both = both.reshape(np_ * span, half)
        for h in range(2):
            sent_back[i, :, :, h * half:(h + 1) * half] = matmul_tn(
                spread[h], both).astype(BF16).reshape(nz, np_, half)
        z_send(2 + i, sent_back.at[i], returned.at[i])

    gateway_back(0)

    @pl.loop(0, inner // step)
    def _(t):
        at = pl.ds(pl.multiple_of(t * step, step), step)
        gw[at, :] = matmul_tn(hid[:, at], rows[1]).astype(BF16)

    store_gw = pltpu.make_async_copy(gw, gw_hbm, store_sem.at[0])
    store_gw.start()
    gateway_back(1)

    z_wait(2, sent_back.at[0], returned.at[0])
    grad_combine = matmul_nt(cot[...], returned[0].reshape(experts, width))
    weight = comb[...]
    through[...] = weight * (
        grad_combine - jnp.sum(weight * grad_combine, axis=1, keepdims=True))
    z_wait(3, sent_back.at[1], returned.at[1])
    grad_rows = returned[1].reshape(experts, width)
    grad_dispatch = matmul_nt(tok[...], grad_rows)
    weight = disp[...]
    grad_logits = (
        weight * (grad_dispatch - jnp.sum(weight * grad_dispatch, axis=0, keepdims=True))
        + through[...]
    ).astype(BF16)
    rsend[...] = matmul(tok_t[...], grad_logits).astype(BF16).reshape(rsend.shape)
    z_send(4, rsend, rmid)
    gt[...] = (
        matmul(weight.astype(BF16), grad_rows) + matmul_nt(grad_logits, rt[...])
    ).astype(BF16)
    store_gt = pltpu.make_async_copy(gt, gt_hbm, store_sem.at[1])
    store_gt.start()
    z_wait(4, rsend, rmid)
    group = rmid[0].astype(F32)
    for k in range(1, nz):
        group = group + rmid[k].astype(F32)
    at_row = lax.broadcasted_iota(jnp.int32, (np_ * pad, np_ * share), 0)
    at_col = lax.broadcasted_iota(jnp.int32, (np_ * pad, np_ * share), 1)
    own = lax.rem(at_row, pad)
    place = jnp.where(
        (at_col == lax.div(at_row, pad) * share + own) & (own < share), 1.0, 0.0).astype(BF16)
    rpad[...] = matmul(place, group.astype(BF16)).astype(BF16).reshape(rpad.shape)
    plane_send(4, rpad, rall, True)
    plane_wait(4, rpad, rall, True)
    total = jnp.sum(rall[...].astype(F32), axis=0)
    gr_ref[...] = total[:share]

    for i in range(2):
        z_drain(i, slots.at[i], gathered.at[i])
        z_drain(2 + i, sent_back.at[i], returned.at[i])
        plane_drain(2 * i, bundles.at[i], arrived.at[i], True)
        plane_drain(2 * i + 1, partial.at[i], partials.at[i], False)
    z_drain(4, rsend, rmid)
    plane_drain(4, rpad, rall, True)
    store_gw.wait()
    store_gt.wait()


def body(np_, tokens, router, w_in, w_out, cotangent):
    tokens, cotangent, w_in, w_out = tokens[0], cotangent[0], w_in[0], w_out[0]
    count, width = tokens.shape
    experts = router.shape[1]
    inner = w_in.shape[1]
    nz = experts // np_
    nq = 2 * np_
    span = 2 * nz
    half = width // 2
    share = width // experts
    pad = -(-share // 16) * 16
    vm = pltpu.VMEM
    anywhere = pl.BlockSpec(memory_space=pl.ANY)
    gt, gw, gr = pl.pallas_call(
        functools.partial(kernel, nz, np_, share, pad),
        out_shape=(
            jax.ShapeDtypeStruct((count, width), BF16),
            jax.ShapeDtypeStruct((inner, width), BF16),
            jax.ShapeDtypeStruct((share, experts), F32),
        ),
        in_specs=[anywhere] * 5,
        out_specs=(anywhere, anywhere, pl.BlockSpec(memory_space=pltpu.VMEM)),
        scratch_shapes=[
            vm((count, width), BF16), vm(router.shape, BF16), vm(w_in.shape, BF16),
            vm(w_out.shape, BF16), vm((count, width), BF16), vm((width, count), BF16),
            vm((count, experts), F32), vm((count, experts), F32), vm((count, experts), F32),
            vm((2, nz, np_, width), BF16), vm((2, nz, np_, width), BF16),
            vm((2, np_, span, half), BF16), vm((2, nq, span, half), BF16),
            vm((2, nq * nz, width), BF16),
            vm((nq * nz, inner), BF16), vm((nq * nz, inner), F32), vm((nq * nz, inner), BF16),
            vm((nq, span, half), F32), vm((2, nq, span, half), BF16),
            vm((2, nq, span, half), BF16),
            vm((2, nz, np_, width), BF16), vm((2, nz, np_, width), BF16),
            vm((nz, np_ * share, experts), BF16), vm((nz, np_ * share, experts), BF16),
            vm((np_, pad, experts), BF16), vm((nq, pad, experts), BF16),
            vm((inner, width), BF16), vm((count, width), BF16),
            pltpu.SemaphoreType.DMA((5,)), pltpu.SemaphoreType.DMA((2,)),
            pltpu.SemaphoreType.DMA((5, nz)), pltpu.SemaphoreType.DMA((5, nz)),
            pltpu.SemaphoreType.DMA((5, nq)), pltpu.SemaphoreType.DMA((5, nq)),
        ],
        compiler_params=pltpu.CompilerParams(
            collective_id=0, has_side_effects=True, vmem_limit_bytes=50 * 1024 * 1024),
    )(tokens, router, w_in, w_out, cotangent)
    return gt[None], gw[None], gr


def solution(mesh, plane=PLANE):
    placed = (
        P(("expert", "replica"), None, None),
        P(),
        P("expert", None, "replica"),
        P("expert", "replica", None),
        P(("expert", "replica"), None, None),
    )
    return jax.shard_map(
        functools.partial(body, plane),
        mesh=mesh,
        in_specs=placed,
        out_specs=(
            P(("expert", "replica"), None, None),
            P("expert", "replica", None),
            P("expert", None),
        ),
        check_vma=False,
    )
```

time: 870 us -> 95.4 us (0.11)
  blocking collectives: 671 us -> 0 us
  Pallas kernels: 0 us -> 86 us
  waiting for transfers between devices: 59.6 us -> 0 us
  starting transfers between devices: 48.7 us -> 0 us
  matrix products: 26.4 us -> 0 us
  local copies, waits for them, and re-layouts: 28.5 us -> 8.42 us
  other arithmetic: 14.8 us -> 0 us
  between operations: 14.6 us -> 0.65 us
    unnamed x1 -> x0, blocking collectives: 651 us -> none
    pallas_call x0 -> x1, Pallas kernels: none -> 86 us  [body(): pl.pallas_call(functools.partial(kernel, nz, np_, share, pad), out_shape=...]
    all_to_all x4 -> x0, starting transfers between devices: 48.4 us -> none  [the longest x1 16.8 us: body(): lax.all_to_all(slot_in, 'expert', split_axis=1, concat_axis=0, tiled=True)]
    psum x1 -> x0, waiting for transfers between devices: 28.2 us -> none  [body(): lax.psum(router_term.astype(jnp.bfloat16), 'replica').astype(jnp.float32)]
    dot_general x12 -> x0, matrix products: 26.4 us -> none  [the longest x1 5.37 us: body(): jnp.einsum('rf,df->rd', picked, first_weight, preferred_element_type=jnp....]
    all_gather x2 -> x0, blocking collectives: 19.5 us -> none  [the longest x1 10.7 us: body(): both_rows = lax.all_gather(slot_rows, 'replica', axis=0, tiled=True)]
    all_to_all x4 -> x0, waiting for transfers between devices: 17.2 us -> none  [the longest x1 8.06 us: body(): lax.all_to_all(slot_in, 'expert', split_axis=1, concat_axis=0, tiled=True)]
    unnamed x28 -> x9, local copies, waits for them, and re-layouts: 23.6 us -> 8.42 us
  transfers between devices with their start and end apart: 7 -> 0, of which waited for: 6 -> 0; matrix products, arithmetic and copies ran while one was open for 6% -> 0% of each run, Pallas kernels for 0% -> 0%
where the time goes in v2:
time: 95.4 us; the launch traced here: 95.1 us
  Pallas kernels  86 us (90%)
  local copies, waits for them, and re-layouts  8.42 us (9%)
    pallas_call x1, Pallas kernels, body(): pl.pallas_call(functools.partial(kernel, nz, np_, share, pad), out_shape=...  86 us
    unnamed x9, local copies, waits for them, and re-layouts  8.42 us

profile of v2, /device:TPU:1, one launch (start us, length us, event | category | flops | bytes accessed | tf_op | source)
XLA Modules:
  0.0 95.1 jit_solution(11471811228608353870)
XLA Ops:
  0.6 0.0 copy-start
  0.6 1.1 %copy-done = bf16[1,256,1280]{2,1,0:T(8,128)(2,1)S(1)} copy-done((bf16[1,256,1280]{2,1,0:T(8,128)(2,1)S(1)}, bf16[1,256,1280]{2,1,0:T(8,128)(2,1)}, u32[]{:S(2)}) %copy-start) | copy-done | bytes 655384
  1.7 0.0 copy-start.1
  1.7 1.1 %copy-done.1 = bf16[1,256,1280]{2,1,0:T(8,128)(2,1)S(1)} copy-done((bf16[1,256,1280]{2,1,0:T(8,128)(2,1)S(1)}, bf16[1,256,1280]{2,1,0:T(8,128)(2,1)}, u32[]{:S(2)}) %copy-start.1) | copy-done | bytes 655384
  2.8 0.0 copy-start.2
  2.8 1.0 %copy-done.2 = bf16[1280,128]{1,0:T(8,128)(2,1)S(1)} copy-done((bf16[1280,128]{1,0:T(8,128)(2,1)S(1)}, bf16[1280,128]{1,0:T(8,128)(2,1)}, u32[]{:S(2)}) %copy-start.2) | copy-done | bytes 327704
  3.8 86.0 %shard_map.76 = (bf16[256,1280]{1,0:T(8,128)(2,1)S(1)}, bf16[1280,1280]{1,0:T(8,128)(2,1)}, f32[10,128]{1,0:T(8,128)S(1)}) custom-call(bf16[256,1280]{1,0:T(8,128)(2,1)S(1)} %bitcast.7, bf16[1280,128]{1,0:T(8,128)(2,1)S(1)} %copy-done.2, bf16[1280,1280]{1,0:T(8,128)(2,1)} %bitcast.10, bf16[1280,1280]{1,0:T(8,128)(2,1)} %bitcast.11, bf16[256,1280]{1,0:T(8,128)(2,1)S(1)} %bitcast.8), custom_call_target="tpu_custom_call" | custom-call | tf_op jit(solution)/shard_map/pallas_call | solution.py:288
  89.8 0.8 copy.11
  90.7 3.8 %copy.12 = bf16[1,1280,1280]{2,1,0:T(8,128)(2,1)} copy(bf16[1,1280,1280]{2,1,0:T(8,128)(2,1)} %bitcast.9) | data formatting | bytes 6553600
  94.5 0.6 copy.13
Async XLA Ops:
  0.6 1.1 %copy-start = (bf16[1,256,1280]{2,1,0:T(8,128)(2,1)S(1)}, bf16[1,256,1280]{2,1,0:T(8,128)(2,1)}, u32[]{:S(2)}) copy-start(bf16[1,256,1280]{2,1,0:T(8,128)(2,1)} %param.5) | copy-start | bytes 1966084
  1.7 1.1 %copy-start.1 = (bf16[1,256,1280]{2,1,0:T(8,128)(2,1)S(1)}, bf16[1,256,1280]{2,1,0:T(8,128)(2,1)}, u32[]{:S(2)}) copy-start(bf16[1,256,1280]{2,1,0:T(8,128)(2,1)} %param.9) | copy-start | bytes 1966084
  2.8 1.0 %copy-start.2 = (bf16[1280,128]{1,0:T(8,128)(2,1)S(1)}, bf16[1280,128]{1,0:T(8,128)(2,1)}, u32[]{:S(2)}) copy-start(bf16[1280,128]{1,0:T(8,128)(2,1)} %rt_hbm.1) | copy-start | bytes 983044

commit v3 on v0

v3 whole, which is shorter than its diff:
```python
import functools

import jax
import jax.numpy as jnp
from jax import lax
from jax.experimental import pallas as pl
from jax.experimental.pallas import tpu as pltpu
from jax.sharding import PartitionSpec as P

F32 = jnp.float32
BF16 = jnp.bfloat16
MESH = pl.DeviceIdType.MESH
PLANE = 16
COLUMNS = 256


def matmul(a, b):
    return jnp.dot(a, b, preferred_element_type=F32)


def matmul_nt(a, b):
    return lax.dot_general(a, b, (((1,), (1,)), ((), ())), preferred_element_type=F32)


def matmul_tn(a, b):
    return lax.dot_general(a, b, (((0,), (0,)), ((), ())), preferred_element_type=F32)


def softmax(logits, axis):
    raised = jnp.exp(logits - jnp.max(logits, axis=axis, keepdims=True))
    return raised / jnp.sum(raised, axis=axis, keepdims=True)


def kernel(
    nz, np_, share, cols, pad, tall,
    tok_hbm, rt_hbm, win_hbm, wout_hbm, cot_hbm,
    gt, gw, gr,
    tok, rt, win, wout, cot, tok_p,
    disp, comb, disp_t, comb_t, grad_c, grad_d,
    slots, gathered, bundles, arrived, partial, partials, sent_back, returned,
    regroup, regroup_t, xb, pre, gh, hid, gpre, grad_rows,
    rsend, rall, rpart, rfin,
    load_sem, fz_s, fz_r, fp_s, fp_r, bp_s, bp_r, bz_s, bz_r, rp_s, rp_r, rf_s, rf_r,
):
    e = lax.axis_index("expert")
    r = lax.axis_index("replica")
    z = lax.div(e, np_)
    p = lax.rem(e, np_)
    nq = 2 * np_
    q = r * np_ + p
    experts = nz * np_
    span = 2 * nz
    wide = 2 * np_
    width = tok.shape[1]
    inner = hid.shape[1]
    chunks = width // cols
    step = 256 if inner % 256 == 0 else inner
    tiles = inner // step
    upper = nz // 2

    def z_peer(k):
        far = lax.div(k + 1, 2)
        far = far + (1 - lax.rem(k, 2)) * (nz - 2 * far)
        return lax.rem(z + far, nz)

    def plane_peer(k):
        return lax.rem(q + k, nq)

    def plane_device(other):
        return (z * np_ + lax.rem(other, np_), lax.div(other, np_))

    loads = [
        pltpu.make_async_copy(src, dst, load_sem.at[i])
        for i, (src, dst) in enumerate(
            ((tok_hbm, tok), (rt_hbm, rt), (cot_hbm, cot), (win_hbm, win), (wout_hbm, wout)))
    ]
    for load in loads:
        load.start()

    barrier = pltpu.get_barrier_semaphore()

    @pl.loop(1, nz)
    def _(k):
        other = z_peer(k) * np_ + p
        pl.semaphore_signal(barrier, inc=1, device_id=(other, r), device_id_type=MESH)
        pl.semaphore_signal(barrier, inc=1, device_id=(other, 1 - r), device_id_type=MESH)

    @pl.loop(1, nq)
    def _(k):
        pl.semaphore_signal(
            barrier, inc=1, device_id=plane_device(plane_peer(k)), device_id_type=MESH)

    def z_send(src, dst, s, t):
        @pl.loop(1, nz)
        def _(k):
            other = z_peer(k)
            pltpu.make_async_remote_copy(
                src_ref=src.at[other], dst_ref=dst.at[z], send_sem=s, recv_sem=t,
                device_id=(other * np_ + p, r), device_id_type=MESH).start()
        dst[z] = src[z]

    def plane_send(src, dst, s, t, fold):
        @pl.loop(1, nq)
        def _(k):
            other = plane_peer(k)
            pltpu.make_async_remote_copy(
                src_ref=src.at[lax.rem(other, np_) if fold else other], dst_ref=dst.at[q],
                send_sem=s, recv_sem=t, device_id=plane_device(other),
                device_id_type=MESH).start()
        dst[q] = src[p if fold else q]

    def all_of(ref, count, s, t):
        part = ref.at[pl.ds(0, count)]
        return pltpu.make_async_remote_copy(
            src_ref=part, dst_ref=part, send_sem=s, recv_sem=t,
            device_id=plane_device(plane_peer(1)), device_id_type=MESH)

    def columns(c):
        return pl.ds(pl.multiple_of(c * cols, cols), cols)

    def hidden_units(t):
        return pl.ds(pl.multiple_of(t * step, step), step)

    pre[...] = jnp.zeros_like(pre)
    gh[...] = jnp.zeros_like(gh)
    grad_c[...] = jnp.zeros_like(grad_c)
    grad_d[...] = jnp.zeros_like(grad_d)
    loads[0].wait()
    loads[1].wait()
    logits = matmul(tok[...], rt[...])
    dispatch = softmax(logits, 0)
    disp[...] = dispatch
    disp_t[...] = dispatch.T.astype(BF16)
    combine = softmax(logits, 1)
    comb[...] = combine
    comb_t[...] = combine.T.astype(BF16)
    loads[2].wait()
    pl.semaphore_wait(barrier, 2 * (nz - 1) + nq - 1)

    @pl.loop(0, chunks)
    def _(c):
        at = columns(c)
        slots[c, :, :np_, :] = matmul(disp_t[...], tok[:, at]).astype(BF16).reshape(
            nz, np_, cols)
        slots[c, :, np_:, :] = matmul(comb_t[...], cot[:, at]).astype(BF16).reshape(
            nz, np_, cols)
        z_send(slots.at[c], gathered.at[c], fz_s.at[c], fz_r.at[c])

    at_row = lax.broadcasted_iota(jnp.int32, (np_ * span, nz * wide), 0)
    at_col = lax.broadcasted_iota(jnp.int32, (np_ * span, nz * wide), 1)
    inside = lax.rem(at_col, wide)
    regroup[...] = jnp.where(
        at_row == lax.rem(inside, np_) * span + lax.div(inside, np_) * nz
        + lax.div(at_col, wide), 1.0, 0.0).astype(BF16)
    inside = lax.rem(at_row, wide)
    regroup_t[...] = jnp.where(
        at_col == lax.rem(inside, np_) * span + lax.div(inside, np_) * nz
        + lax.div(at_row, wide), 1.0, 0.0).astype(BF16)

    def gateway(c):
        all_of(gathered.at[c], nz - 1, fz_s.at[c], fz_r.at[c]).wait_recv()
        bundles[c] = matmul(
            regroup[...], gathered[c].reshape(nz * wide, cols)
        ).astype(BF16).reshape(np_, span, cols)
        plane_send(bundles.at[c], arrived.at[c], fp_s.at[c], fp_r.at[c], True)

    many = tok_p.shape[0] // 4

    def spread_tokens(t):
        row = lax.broadcasted_iota(jnp.int32, (many, width), 0) + t * many
        col = lax.broadcasted_iota(jnp.int32, (many, width), 1)
        to = lax.div(row, tall)
        row = row - to * tall
        level = jnp.zeros_like(row)
        for k in range(1, upper):
            level = level + jnp.where(row >= k * share, 1, 0)
        level_r = lax.div(to, np_)
        source = (
            (level_r * upper + level) * (np_ * share) + (to - level_r * np_) * share
            + row - level * share)
        pick = jnp.where((col == source) & (row < upper * share), 1.0, 0.0).astype(BF16)
        tok_p[pl.ds(pl.multiple_of(t * many, many), many), :] = matmul_nt(
            pick, tok[...]).astype(BF16)

    def expert_rows(c):
        all_of(arrived.at[c], nq - 1, fp_s.at[c], fp_r.at[c]).wait_recv()
        block = arrived[c].astype(F32)
        xa = block[:, :nz, :].reshape(nq * nz, cols).astype(BF16)
        own = block[:, nz:, :].reshape(nq * nz, cols).astype(BF16)
        xb[:, columns(c)] = own
        return xa, own

    def accumulate(c):
        xa, own = expert_rows(c)

        @pl.loop(0, tiles)
        def _(t):
            at = hidden_units(t)
            pre[:, at] += matmul(xa, win[columns(c), at])
            gh[:, at] += matmul_nt(own, wout[at, columns(c)])

    lag = min(2, chunks - 1)

    @pl.loop(0, lag)
    def _(c):
        gateway(c)
        spread_tokens(2 * c)
        spread_tokens(2 * c + 1)

    if lag == 1:
        spread_tokens(2)
        spread_tokens(3)
    loads[3].wait()
    loads[4].wait()

    @pl.loop(lag, chunks)
    def _(c):
        gateway(c)
        accumulate(c - lag)

    @pl.loop(chunks - lag, chunks - 1)
    def _(c):
        accumulate(c)

    last = chunks - 1
    xa, own = expert_rows(last)

    @pl.loop(0, tiles)
    def _(t):
        at = hidden_units(t)
        act = pre[:, at] + matmul(xa, win[columns(last), at])
        lower = 0.5 * (1.0 + lax.erf(act * 0.7071067811865476))
        hid[:, at] = (act * lower).astype(BF16)
        slope = lower + act * jnp.exp(-0.5 * act * act) * 0.3989422804014327
        grad = gh[:, at] + matmul_nt(own, wout[at, columns(last)])
        gpre[:, at] = (grad * slope).astype(BF16)

    @pl.loop(0, chunks)
    def _(c):
        at = columns(c)
        out = matmul(hid[...], wout[:, at]).reshape(nq, nz, cols)
        back = matmul_nt(gpre[...], win[at, :]).reshape(nq, nz, cols)
        partial[c] = jnp.concatenate([out, back], axis=1).astype(BF16)
        plane_send(partial.at[c], partials.at[c], bp_s.at[c], bp_r.at[c], False)

    def gateway_back(c):
        all_of(partials.at[c], nq - 1, bp_s.at[c], bp_r.at[c]).wait_recv()
        both = (partials[c, :np_].astype(F32) + partials[c, np_:].astype(F32)).astype(BF16)
        sent_back[c] = matmul(
            regroup_t[...], both.reshape(np_ * span, cols)
        ).astype(BF16).reshape(nz, wide, cols)
        z_send(sent_back.at[c], returned.at[c], bz_s.at[c], bz_r.at[c])

    def image_rows(c):
        all_of(returned.at[c], nz - 1, bz_s.at[c], bz_r.at[c]).wait_recv()
        at = columns(c)
        block = returned[c]
        grad_c[...] += matmul_nt(cot[:, at], block[:, :np_, :].reshape(experts, cols))
        own = block[:, np_:, :].reshape(experts, cols)
        grad_rows[:, at] = own
        grad_d[...] += matmul_nt(tok[:, at], own)

    def weight_rows(t):
        at = hidden_units(t)
        gw[at, :] = matmul_tn(hid[:, at], xb[...]).astype(BF16)

    def forward_sent(c):
        all_of(slots.at[c], nz - 1, fz_s.at[c], fz_r.at[c]).wait_send()
        all_of(arrived.at[c], nq - 1, fp_s.at[c], fp_r.at[c]).wait_send()

    @pl.loop(0, tiles)
    def _(t):
        weight_rows(t)

    @pl.loop(0, lag)
    def _(c):
        gateway_back(c)
        forward_sent(c)

    @pl.loop(lag, chunks)
    def _(c):
        gateway_back(c)
        forward_sent(c)
        image_rows(c - lag)

    @pl.loop(chunks - lag, chunks)
    def _(c):
        image_rows(c)

    got = grad_c[...]
    weight = comb[...]
    through = weight * (got - jnp.sum(weight * got, axis=1, keepdims=True))
    got = grad_d[...]
    weight = disp[...]
    grad_logits = (
        weight * (got - jnp.sum(weight * got, axis=0, keepdims=True)) + through
    ).astype(BF16)
    rsend[...] = matmul(tok_p[...], grad_logits).astype(BF16).reshape(rsend.shape)
    plane_send(rsend, rall, rp_s, rp_r, False)
    gt[...] = (
        matmul(weight.astype(BF16), grad_rows[...]) + matmul_nt(grad_logits, rt[...])
    ).astype(BF16)

    @pl.loop(0, chunks)
    def _(c):
        all_of(partials.at[c], nq - 1, bp_s.at[c], bp_r.at[c]).wait_send()
        all_of(returned.at[c], nz - 1, bz_s.at[c], bz_r.at[c]).wait_send()

    at_row = lax.broadcasted_iota(jnp.int32, (upper * pad, tall), 0)
    at_col = lax.broadcasted_iota(jnp.int32, (upper * pad, tall), 1)
    level = lax.div(at_row, pad)
    own = at_row - level * pad
    place = jnp.where(
        (at_col == level * share + own) & (own < share), 1.0, 0.0).astype(BF16)
    all_of(rall, nq - 1, rp_s, rp_r).wait_recv()
    group = jnp.sum(rall[...].astype(F32), axis=0).astype(BF16)
    rpart[...] = matmul(place, group).astype(BF16).reshape(rpart.shape)
    mine = lax.div(z, upper)

    def hand_over(t):
        level, other = lax.div(t, 2), lax.rem(t, 2)
        to = r * upper + level
        copy = pltpu.make_async_remote_copy(
            src_ref=rpart.at[level], dst_ref=rfin.at[z], send_sem=rf_s.at[t],
            recv_sem=rf_r.at[z], device_id=(to * np_ + p, other), device_id_type=MESH)
        return copy, (to != z) | (other != r)

    @pl.loop(0, nz)
    def _(t):
        copy, away = hand_over(t)

        @pl.when(away)
        def _():
            copy.start()

        @pl.when(jnp.logical_not(away))
        def _():
            rfin[z] = rpart[lax.div(t, 2)]

    @pl.loop(0, nz)
    def _(k):
        @pl.when((k != z) | (mine != r))
        def _():
            pltpu.make_async_remote_copy(
                src_ref=rpart.at[0], dst_ref=rfin.at[k], send_sem=rf_s.at[0],
                recv_sem=rf_r.at[k], device_id=plane_device(plane_peer(1)),
                device_id_type=MESH).wait_recv()

    gr[...] = jnp.sum(rfin[...].astype(F32), axis=0)[:share]
    all_of(rsend, nq - 1, rp_s, rp_r).wait_send()

    @pl.loop(0, nz)
    def _(t):
        copy, away = hand_over(t)

        @pl.when(away)
        def _():
            copy.wait_send()


def write_out(gt, gw, gr, gt_hbm, gw_hbm, gr_hbm, sem):
    moves = [
        pltpu.make_async_copy(src, dst, sem.at[i])
        for i, (src, dst) in enumerate(((gw, gw_hbm), (gt, gt_hbm), (gr, gr_hbm)))
    ]
    for move in moves:
        move.start()
    for move in moves:
        move.wait()


def body(np_, cols, tokens, router, w_in, w_out, cotangent):
    count, width = tokens.shape[1:]
    experts = router.shape[1]
    inner = w_in.shape[2]
    nz = experts // np_
    nq = 2 * np_
    span = 2 * nz
    wide = 2 * np_
    share = width // experts
    pad = -(-share // 16) * 16
    tall = -(-share * (nz // 2) // 16) * 16
    chunks = width // cols
    vm = pltpu.VMEM
    dma = pltpu.SemaphoreType.DMA
    whole = pl.BlockSpec(memory_space=vm)
    far = pl.BlockSpec(memory_space=pltpu.HBM)
    operands = [
        pltpu.with_memory_space_constraint(a, pltpu.HBM)
        for a in (tokens[0], router, w_in[0], w_out[0], cotangent[0])
    ]
    outs = pl.pallas_call(
        functools.partial(kernel, nz, np_, share, cols, pad, tall),
        out_shape=(vm((count, width), BF16), vm((inner, width), BF16), vm((share, experts), F32)),
        in_specs=[far] * 5,
        out_specs=(whole, whole, whole),
        scratch_shapes=[
            vm((count, width), BF16), vm(router.shape, BF16), vm((width, inner), BF16),
            vm((inner, width), BF16), vm((count, width), BF16), vm((nq * tall, count), BF16),
            vm((count, experts), F32), vm((count, experts), F32),
            vm((experts, count), BF16), vm((experts, count), BF16),
            vm((count, experts), F32), vm((count, experts), F32),
            vm((chunks, nz, wide, cols), BF16), vm((chunks, nz, wide, cols), BF16),
            vm((chunks, np_, span, cols), BF16), vm((chunks, nq, span, cols), BF16),
            vm((chunks, nq, span, cols), BF16), vm((chunks, nq, span, cols), BF16),
            vm((chunks, nz, wide, cols), BF16), vm((chunks, nz, wide, cols), BF16),
            vm((np_ * span, nz * wide), BF16), vm((nz * wide, np_ * span), BF16),
            vm((nq * nz, width), BF16), vm((nq * nz, inner), F32), vm((nq * nz, inner), F32),
            vm((nq * nz, inner), BF16), vm((nq * nz, inner), BF16), vm((experts, width), BF16),
            vm((nq, tall, experts), BF16), vm((nq, tall, experts), BF16),
            vm((nz // 2, pad, experts), BF16), vm((nz, pad, experts), BF16),
            dma((5,)), dma((chunks,)), dma((chunks,)), dma((chunks,)), dma((chunks,)),
            dma((chunks,)), dma((chunks,)), dma((chunks,)), dma((chunks,)),
            dma(()), dma(()), dma((nz,)), dma((nz,)),
        ],
        compiler_params=pltpu.CompilerParams(
            collective_id=0, has_side_effects=True, vmem_limit_bytes=48 * 1024 * 1024),
    )(*operands)
    gt, gw, gr = pl.pallas_call(
        write_out,
        out_shape=[jax.ShapeDtypeStruct(a.shape, a.dtype) for a in outs],
        in_specs=[whole] * 3,
        out_specs=[far] * 3,
        scratch_shapes=[dma((3,))],
        compiler_params=pltpu.CompilerParams(vmem_limit_bytes=8 * 1024 * 1024),
    )(*[pltpu.with_memory_space_constraint(a, vm) for a in outs])
    return gt[None], gw[None], gr


def solution(mesh, plane=PLANE, cols=COLUMNS):
    placed = (
        P(("expert", "replica"), None, None),
        P(),
        P("expert", None, "replica"),
        P("expert", "replica", None),
        P(("expert", "replica"), None, None),
    )
    return jax.shard_map(
        functools.partial(body, plane, cols),
        mesh=mesh,
        in_specs=placed,
        out_specs=(
            P(("expert", "replica"), None, None),
            P("expert", "replica", None),
            P("expert", None),
        ),
        check_vma=False,
    )
```

time: 870 us -> 79.5 us (0.09)
  blocking collectives: 671 us -> 0 us
  Pallas kernels: 0 us -> 78.7 us
  waiting for transfers between devices: 59.6 us -> 0 us
  starting transfers between devices: 48.7 us -> 0 us
  local copies, waits for them, and re-layouts: 28.5 us -> 0 us
  matrix products: 26.4 us -> 0 us
  other arithmetic: 14.8 us -> 0 us
  between operations: 14.6 us -> 0.64 us
    unnamed x1 -> x0, blocking collectives: 651 us -> none
    pallas_call x0 -> x2, Pallas kernels: none -> 78.7 us  [the longest x1 76.8 us: body(): pl.pallas_call(functools.partial(kernel, nz, np_, share, cols, pad, tall)...]
    all_to_all x4 -> x0, starting transfers between devices: 48.4 us -> none  [the longest x1 16.8 us: body(): lax.all_to_all(slot_in, 'expert', split_axis=1, concat_axis=0, tiled=True)]
    psum x1 -> x0, waiting for transfers between devices: 28.2 us -> none  [body(): lax.psum(router_term.astype(jnp.bfloat16), 'replica').astype(jnp.float32)]
    dot_general x12 -> x0, matrix products: 26.4 us -> none  [the longest x1 5.37 us: body(): jnp.einsum('rf,df->rd', picked, first_weight, preferred_element_type=jnp....]
    unnamed x28 -> x0, local copies, waits for them, and re-layouts: 23.6 us -> none
    all_gather x2 -> x0, blocking collectives: 19.5 us -> none  [the longest x1 10.7 us: body(): both_rows = lax.all_gather(slot_rows, 'replica', axis=0, tiled=True)]
    all_to_all x4 -> x0, waiting for transfers between devices: 17.2 us -> none  [the longest x1 8.06 us: body(): lax.all_to_all(slot_in, 'expert', split_axis=1, concat_axis=0, tiled=True)]
  transfers between devices with their start and end apart: 7 -> 0, of which waited for: 6 -> 0; matrix products, arithmetic and copies ran while one was open for 6% -> 0% of each run, Pallas kernels for 0% -> 0%
where the time goes in v3:
time: 79.5 us; the launch traced here: 79.4 us
  Pallas kernels  78.7 us (99%)
    pallas_call x1, Pallas kernels, body(): pl.pallas_call(functools.partial(kernel, nz, np_, share, cols, pad, tall)...  76.8 us
    pallas_call x1, Pallas kernels, body(): pl.pallas_call(write_out, out_shape=[jax.ShapeDtypeStruct(a.shape, a.dtyp...  1.95 us

profile of v3, /device:TPU:1, one launch (start us, length us, event | category | flops | bytes accessed | tf_op | source)
XLA Modules:
  0.0 79.4 jit_solution(1254508240531169266)
XLA Ops:
  0.6 76.8 %shard_map.76 = (bf16[256,1280]{1,0:T(8,128)(2,1)S(1)}, bf16[1280,1280]{1,0:T(8,128)(2,1)S(1)}, f32[10,128]{1,0:T(8,128)S(1)}) custom-call(bf16[256,1280]{1,0:T(8,128)(2,1)} %bitcast.8, bf16[1280,128]{1,0:T(8,128)(2,1)} %rt_hbm.1, bf16[1280,1280]{1,0:T(8,128)(2,1)} %bitcast.6, bf16[1280,1280]{1,0:T(8,128)(2,1)} %bitcast.7, bf16[256,1280]{1,0:T(8,128)(2,1)} %bitcast.9), custom_call_target="tpu_custom_call" | custom-call | tf_op jit(solution)/shard_map/pallas_call | solution.py:392
  77.4 1.9 %shard_map.77 = (bf16[256,1280]{1,0:T(8,128)(2,1)}, bf16[1280,1280]{1,0:T(8,128)(2,1)}, f32[10,128]{1,0:T(8,128)}) custom-call(bf16[256,1280]{1,0:T(8,128)(2,1)S(1)} %get-tuple-element.9.gt, bf16[1280,1280]{1,0:T(8,128)(2,1)S(1)} %get-tuple-element.10.gw, f32[10,128]{1,0:T(8,128)S(1)} %get-tuple-element.11.gr), custom_call_target="tpu_custom_call" | custom-call | tf_op jit(solution)/shard_map/pallas_call | solution.py:419

commit v4 on v3

--- a/solution.py
+++ b/solution.py
@@ -36,9 +36,9 @@
     tok_hbm, rt_hbm, win_hbm, wout_hbm, cot_hbm,
     gt, gw, gr,
     tok, rt, win, wout, cot, tok_p,
-    disp, comb, disp_t, comb_t, grad_c, grad_d,
+    disp, comb, disp_t, comb_t, through, grad_c, grad_d,
     slots, gathered, bundles, arrived, partial, partials, sent_back, returned,
-    regroup, regroup_t, xb, pre, gh, hid, gpre, grad_rows,
+    regroup, regroup_t, xa, xb, slope, hid, gpre, grad_rows,
     rsend, rall, rpart, rfin,
     load_sem, fz_s, fz_r, fp_s, fp_r, bp_s, bp_r, bz_s, bz_r, rp_s, rp_r, rf_s, rf_r,
 ):
@@ -54,20 +54,23 @@
     width = tok.shape[1]
     inner = hid.shape[1]
     chunks = width // cols
-    step = 256 if inner % 256 == 0 else inner
-    tiles = inner // step
+    half = cols // 2
+    step = inner // chunks
+    tiles = chunks
     upper = nz // 2
 
+    def below(value, limit):
+        return lax.bitwise_and(value, jnp.int32(limit - 1))
+
     def z_peer(k):
-        far = lax.div(k + 1, 2)
-        far = far + (1 - lax.rem(k, 2)) * (nz - 2 * far)
-        return lax.rem(z + far, nz)
+        far = (k + 1) // 2
+        return below(z + (far if k % 2 else nz - far), nz)
 
     def plane_peer(k):
-        return lax.rem(q + k, nq)
+        return below(q + k, nq)
 
     def plane_device(other):
-        return (z * np_ + lax.rem(other, np_), lax.div(other, np_))
+        return (z * np_ + below(other, np_), lax.div(other, np_))
 
     loads = [
         pltpu.make_async_copy(src, dst, load_sem.at[i])
@@ -79,20 +82,17 @@
 
     barrier = pltpu.get_barrier_semaphore()
 
-    @pl.loop(1, nz)
-    def _(k):
+    for k in range(1, nz):
         other = z_peer(k) * np_ + p
         pl.semaphore_signal(barrier, inc=1, device_id=(other, r), device_id_type=MESH)
         pl.semaphore_signal(barrier, inc=1, device_id=(other, 1 - r), device_id_type=MESH)
 
-    @pl.loop(1, nq)
-    def _(k):
+    for k in range(1, nq):
         pl.semaphore_signal(
             barrier, inc=1, device_id=plane_device(plane_peer(k)), device_id_type=MESH)
 
     def z_send(src, dst, s, t):
-        @pl.loop(1, nz)
-        def _(k):
+        for k in range(1, nz):
             other = z_peer(k)
             pltpu.make_async_remote_copy(
                 src_ref=src.at[other], dst_ref=dst.at[z], send_sem=s, recv_sem=t,
@@ -100,11 +100,10 @@
         dst[z] = src[z]
 
     def plane_send(src, dst, s, t, fold):
-        @pl.loop(1, nq)
-        def _(k):
+        for k in range(1, nq):
             other = plane_peer(k)
             pltpu.make_async_remote_copy(
-                src_ref=src.at[lax.rem(other, np_) if fold else other], dst_ref=dst.at[q],
+                src_ref=src.at[below(other, np_) if fold else other], dst_ref=dst.at[q],
                 send_sem=s, recv_sem=t, device_id=plane_device(other),
                 device_id_type=MESH).start()
         dst[q] = src[p if fold else q]
@@ -121,8 +120,6 @@
     def hidden_units(t):
         return pl.ds(pl.multiple_of(t * step, step), step)
 
-    pre[...] = jnp.zeros_like(pre)
-    gh[...] = jnp.zeros_like(gh)
     grad_c[...] = jnp.zeros_like(grad_c)
     grad_d[...] = jnp.zeros_like(grad_d)
     loads[0].wait()
@@ -131,20 +128,26 @@
     dispatch = softmax(logits, 0)
     disp[...] = dispatch
     disp_t[...] = dispatch.T.astype(BF16)
+    pl.semaphore_wait(barrier, 2 * (nz - 1) + nq - 1)
+
+    def slot_rows(c, weights, values):
+        out = matmul(weights[...], values).astype(BF16)
+        slots[c, :, :np_, :] = out[:, :half].reshape(nz, np_, half)
+        slots[c, :, np_:, :] = out[:, half:].reshape(nz, np_, half)
+        z_send(slots.at[c], gathered.at[c], fz_s.at[c], fz_r.at[c])
+
+    @pl.loop(0, chunks)
+    def _(c):
+        slot_rows(c, disp_t, tok[:, columns(c)])
+
     combine = softmax(logits, 1)
     comb[...] = combine
     comb_t[...] = combine.T.astype(BF16)
     loads[2].wait()
-    pl.semaphore_wait(barrier, 2 * (nz - 1) + nq - 1)
-
-    @pl.loop(0, chunks)
-    def _(c):
-        at = columns(c)
-        slots[c, :, :np_, :] = matmul(disp_t[...], tok[:, at]).astype(BF16).reshape(
-            nz, np_, cols)
-        slots[c, :, np_:, :] = matmul(comb_t[...], cot[:, at]).astype(BF16).reshape(
-            nz, np_, cols)
-        z_send(slots.at[c], gathered.at[c], fz_s.at[c], fz_r.at[c])
+
+    @pl.loop(0, chunks)
+    def _(c):
+        slot_rows(chunks + c, comb_t, cot[:, columns(c)])
 
     at_row = lax.broadcasted_iota(jnp.int32, (np_ * span, nz * wide), 0)
     at_col = lax.broadcasted_iota(jnp.int32, (np_ * span, nz * wide), 1)
@@ -160,8 +163,8 @@
     def gateway(c):
         all_of(gathered.at[c], nz - 1, fz_s.at[c], fz_r.at[c]).wait_recv()
         bundles[c] = matmul(
-            regroup[...], gathered[c].reshape(nz * wide, cols)
-        ).astype(BF16).reshape(np_, span, cols)
+            regroup[...], gathered[c].reshape(nz * wide, half)
+        ).astype(BF16).reshape(np_, span, half)
         plane_send(bundles.at[c], arrived.at[c], fp_s.at[c], fp_r.at[c], True)
 
     many = tok_p.shape[0] // 4
@@ -185,80 +188,61 @@
     def expert_rows(c):
         all_of(arrived.at[c], nq - 1, fp_s.at[c], fp_r.at[c]).wait_recv()
         block = arrived[c].astype(F32)
-        xa = block[:, :nz, :].reshape(nq * nz, cols).astype(BF16)
-        own = block[:, nz:, :].reshape(nq * nz, cols).astype(BF16)
-        xb[:, columns(c)] = own
-        return xa, own
-
-    def accumulate(c):
-        xa, own = expert_rows(c)
-
-        @pl.loop(0, tiles)
-        def _(t):
-            at = hidden_units(t)
-            pre[:, at] += matmul(xa, win[columns(c), at])
-            gh[:, at] += matmul_nt(own, wout[at, columns(c)])
-
-    lag = min(2, chunks - 1)
-
-    @pl.loop(0, lag)
-    def _(c):
-        gateway(c)
-        spread_tokens(2 * c)
-        spread_tokens(2 * c + 1)
-
-    if lag == 1:
-        spread_tokens(2)
-        spread_tokens(3)
-    loads[3].wait()
-    loads[4].wait()
-
-    @pl.loop(lag, chunks)
-    def _(c):
-        gateway(c)
-        accumulate(c - lag)
-
-    @pl.loop(chunks - lag, chunks - 1)
-    def _(c):
-        accumulate(c)
-
-    last = chunks - 1
-    xa, own = expert_rows(last)
-
-    @pl.loop(0, tiles)
-    def _(t):
+        return jnp.concatenate(
+            [block[:, :nz, :].reshape(nq * nz, half), block[:, nz:, :].reshape(nq * nz, half)],
+            axis=1).astype(BF16)
+
+    def add_input(c):
+        xa[:, columns(c)] = expert_rows(c)
+
+    def add_grad(c):
+        xb[:, columns(c)] = expert_rows(chunks + c)
+
+    def forward_units(t):
         at = hidden_units(t)
-        act = pre[:, at] + matmul(xa, win[columns(last), at])
+        act = matmul(xa[...], win[:, at])
         lower = 0.5 * (1.0 + lax.erf(act * 0.7071067811865476))
         hid[:, at] = (act * lower).astype(BF16)
-        slope = lower + act * jnp.exp(-0.5 * act * act) * 0.3989422804014327
-        grad = gh[:, at] + matmul_nt(own, wout[at, columns(last)])
-        gpre[:, at] = (grad * slope).astype(BF16)
-
-    @pl.loop(0, chunks)
-    def _(c):
-        at = columns(c)
-        out = matmul(hid[...], wout[:, at]).reshape(nq, nz, cols)
-        back = matmul_nt(gpre[...], win[at, :]).reshape(nq, nz, cols)
-        partial[c] = jnp.concatenate([out, back], axis=1).astype(BF16)
+        slope[:, at] = lower + act * jnp.exp(-0.5 * act * act) * 0.3989422804014327
+
+    def backward_units(t):
+        at = hidden_units(t)
+        gpre[:, at] = (matmul_nt(xb[...], wout[at, :]) * slope[:, at]).astype(BF16)
+
+    def send_back(c, out):
+        partial[c] = jnp.concatenate(
+            [out[:, :half].reshape(nq, nz, half), out[:, half:].reshape(nq, nz, half)],
+            axis=1).astype(BF16)
         plane_send(partial.at[c], partials.at[c], bp_s.at[c], bp_r.at[c], False)
+
+    def send_out(c):
+        send_back(c, matmul(hid[...], wout[:, columns(c)]))
+
+    def send_grad(c):
+        send_back(chunks + c, matmul_nt(gpre[...], win[columns(c), :]))
 
     def gateway_back(c):
         all_of(partials.at[c], nq - 1, bp_s.at[c], bp_r.at[c]).wait_recv()
         both = (partials[c, :np_].astype(F32) + partials[c, np_:].astype(F32)).astype(BF16)
         sent_back[c] = matmul(
-            regroup_t[...], both.reshape(np_ * span, cols)
-        ).astype(BF16).reshape(nz, wide, cols)
+            regroup_t[...], both.reshape(np_ * span, half)
+        ).astype(BF16).reshape(nz, wide, half)
         z_send(sent_back.at[c], returned.at[c], bz_s.at[c], bz_r.at[c])
 
     def image_rows(c):
         all_of(returned.at[c], nz - 1, bz_s.at[c], bz_r.at[c]).wait_recv()
-        at = columns(c)
         block = returned[c]
-        grad_c[...] += matmul_nt(cot[:, at], block[:, :np_, :].reshape(experts, cols))
-        own = block[:, np_:, :].reshape(experts, cols)
-        grad_rows[:, at] = own
-        grad_d[...] += matmul_nt(tok[:, at], own)
+        return jnp.concatenate(
+            [block[:, :np_, :].reshape(experts, half), block[:, np_:, :].reshape(experts, half)],
+            axis=1)
+
+    def image_out(c):
+        grad_c[...] += matmul_nt(cot[:, columns(c)], image_rows(c))
+
+    def image_grad(c):
+        rows = image_rows(chunks + c)
+        grad_rows[:, columns(c)] = rows
+        grad_d[...] += matmul_nt(tok[:, columns(c)], rows)
 
     def weight_rows(t):
         at = hidden_units(t)
@@ -268,32 +252,72 @@
         all_of(slots.at[c], nz - 1, fz_s.at[c], fz_r.at[c]).wait_send()
         all_of(arrived.at[c], nq - 1, fp_s.at[c], fp_r.at[c]).wait_send()
 
+    def backward_sent(c):
+        all_of(partials.at[c], nq - 1, bp_s.at[c], bp_r.at[c]).wait_send()
+        all_of(returned.at[c], nz - 1, bz_s.at[c], bz_r.at[c]).wait_send()
+
+    lag = min(3, chunks - 1)
+
+    @pl.loop(0, lag)
+    def _(c):
+        gateway(c)
+        spread_tokens(c)
+
+    for t in range(lag, 4):
+        spread_tokens(t)
+
+    @pl.loop(lag, lag + chunks)
+    def _(c):
+        gateway(c)
+        add_input(c - lag)
+
+    loads[3].wait()
+    loads[4].wait()
+    early = chunks - lag
+    first = -(-tiles // early)
+
+    @pl.loop(0, early)
+    def _(c):
+        @pl.loop(c * first, jnp.minimum((c + 1) * first, tiles))
+        def _(t):
+            forward_units(t)
+
+        gateway(lag + chunks + c)
+
+    @pl.loop(0, chunks)
+    def _(c):
+        send_out(c)
+        add_grad(c)
+
     @pl.loop(0, tiles)
     def _(t):
-        weight_rows(t)
-
-    @pl.loop(0, lag)
-    def _(c):
+        backward_units(t)
+
+    @pl.loop(0, chunks)
+    def _(c):
+        send_grad(c)
         gateway_back(c)
+
+    @pl.loop(0, chunks)
+    def _(c):
+        weight_rows(c)
         forward_sent(c)
-
-    @pl.loop(lag, chunks)
-    def _(c):
-        gateway_back(c)
-        forward_sent(c)
-        image_rows(c - lag)
-
-    @pl.loop(chunks - lag, chunks)
-    def _(c):
-        image_rows(c)
+        forward_sent(chunks + c)
+        image_out(c)
+        gateway_back(chunks + c)
 
     got = grad_c[...]
     weight = comb[...]
-    through = weight * (got - jnp.sum(weight * got, axis=1, keepdims=True))
+    through[...] = weight * (got - jnp.sum(weight * got, axis=1, keepdims=True))
+
+    @pl.loop(0, chunks)
+    def _(c):
+        image_grad(c)
+
     got = grad_d[...]
     weight = disp[...]
     grad_logits = (
-        weight * (got - jnp.sum(weight * got, axis=0, keepdims=True)) + through
+        weight * (got - jnp.sum(weight * got, axis=0, keepdims=True)) + through[...]
     ).astype(BF16)
     rsend[...] = matmul(tok_p[...], grad_logits).astype(BF16).reshape(rsend.shape)
     plane_send(rsend, rall, rp_s, rp_r, False)
@@ -301,10 +325,9 @@
         matmul(weight.astype(BF16), grad_rows[...]) + matmul_nt(grad_logits, rt[...])
     ).astype(BF16)
 
-    @pl.loop(0, chunks)
-    def _(c):
-        all_of(partials.at[c], nq - 1, bp_s.at[c], bp_r.at[c]).wait_send()
-        all_of(returned.at[c], nz - 1, bz_s.at[c], bz_r.at[c]).wait_send()
+    @pl.loop(0, 2 * chunks)
+    def _(c):
+        backward_sent(c)
 
     at_row = lax.broadcasted_iota(jnp.int32, (upper * pad, tall), 0)
     at_col = lax.broadcasted_iota(jnp.int32, (upper * pad, tall), 1)
@@ -380,7 +403,8 @@
     share = width // experts
     pad = -(-share // 16) * 16
     tall = -(-share * (nz // 2) // 16) * 16
-    chunks = width // cols
+    parts = 2 * (width // cols)
+    half = cols // 2
     vm = pltpu.VMEM
     dma = pltpu.SemaphoreType.DMA
     whole = pl.BlockSpec(memory_space=vm)
@@ -398,19 +422,19 @@
             vm((count, width), BF16), vm(router.shape, BF16), vm((width, inner), BF16),
             vm((inner, width), BF16), vm((count, width), BF16), vm((nq * tall, count), BF16),
             vm((count, experts), F32), vm((count, experts), F32),
-            vm((experts, count), BF16), vm((experts, count), BF16),
+            vm((experts, count), BF16), vm((experts, count), BF16), vm((count, experts), F32),
             vm((count, experts), F32), vm((count, experts), F32),
-            vm((chunks, nz, wide, cols), BF16), vm((chunks, nz, wide, cols), BF16),
-            vm((chunks, np_, span, cols), BF16), vm((chunks, nq, span, cols), BF16),
-            vm((chunks, nq, span, cols), BF16), vm((chunks, nq, span, cols), BF16),
-            vm((chunks, nz, wide, cols), BF16), vm((chunks, nz, wide, cols), BF16),
+            vm((parts, nz, wide, half), BF16), vm((parts, nz, wide, half), BF16),
+            vm((parts, np_, span, half), BF16), vm((parts, nq, span, half), BF16),
+            vm((parts, nq, span, half), BF16), vm((parts, nq, span, half), BF16),
+            vm((parts, nz, wide, half), BF16), vm((parts, nz, wide, half), BF16),
             vm((np_ * span, nz * wide), BF16), vm((nz * wide, np_ * span), BF16),
-            vm((nq * nz, width), BF16), vm((nq * nz, inner), F32), vm((nq * nz, inner), F32),
+            vm((nq * nz, width), BF16), vm((nq * nz, width), BF16), vm((nq * nz, inner), F32),
             vm((nq * nz, inner), BF16), vm((nq * nz, inner), BF16), vm((experts, width), BF16),
             vm((nq, tall, experts), BF16), vm((nq, tall, experts), BF16),
             vm((nz // 2, pad, experts), BF16), vm((nz, pad, experts), BF16),
-            dma((5,)), dma((chunks,)), dma((chunks,)), dma((chunks,)), dma((chunks,)),
-            dma((chunks,)), dma((chunks,)), dma((chunks,)), dma((chunks,)),
+            dma((5,)), dma((parts,)), dma((parts,)), dma((parts,)), dma((parts,)),
+            dma((parts,)), dma((parts,)), dma((parts,)), dma((parts,)),
             dma(()), dma(()), dma((nz,)), dma((nz,)),
         ],
         compiler_params=pltpu.CompilerParams(

time: 79.5 us -> 71.8 us (0.903)
  Pallas kernels: 78.7 us -> 71.1 us
    pallas_call x1, Pallas kernels: 76.8 us -> 69.2 us  [body(): pl.pallas_call(functools.partial(kernel, nz, np_, share, cols, pad, tall)...]
where the time goes in v4:
time: 71.8 us
  Pallas kernels  71.1 us (99%)
    pallas_call x1, Pallas kernels, body(): pl.pallas_call(functools.partial(kernel, nz, np_, share, cols, pad, tall)...  69.2 us
    pallas_call x1, Pallas kernels, body(): pl.pallas_call(write_out, out_shape=[jax.ShapeDtypeStruct(a.shape, a.dtyp...  1.95 us

profile of v4, /device:TPU:1, one launch (start us, length us, event | category | flops | bytes accessed | tf_op | source)
XLA Modules:
  0.0 71.8 jit_solution(12668113217113839926)
XLA Ops:
  0.6 69.2 %shard_map.76 = (bf16[256,1280]{1,0:T(8,128)(2,1)S(1)}, bf16[1280,1280]{1,0:T(8,128)(2,1)S(1)}, f32[10,128]{1,0:T(8,128)S(1)}) custom-call(bf16[256,1280]{1,0:T(8,128)(2,1)} %bitcast.8, bf16[1280,128]{1,0:T(8,128)(2,1)} %rt_hbm.1, bf16[1280,1280]{1,0:T(8,128)(2,1)} %bitcast.6, bf16[1280,1280]{1,0:T(8,128)(2,1)} %bitcast.7, bf16[256,1280]{1,0:T(8,128)(2,1)} %bitcast.9), custom_call_target="tpu_custom_call" | custom-call | tf_op jit(solution)/shard_map/pallas_call | solution.py:416
  69.8 1.9 %shard_map.77 = (bf16[256,1280]{1,0:T(8,128)(2,1)}, bf16[1280,1280]{1,0:T(8,128)(2,1)}, f32[10,128]{1,0:T(8,128)}) custom-call(bf16[256,1280]{1,0:T(8,128)(2,1)S(1)} %get-tuple-element.9.gt, bf16[1280,1280]{1,0:T(8,128)(2,1)S(1)} %get-tuple-element.10.gw, f32[10,128]{1,0:T(8,128)S(1)} %get-tuple-element.11.gr), custom_call_target="tpu_custom_call" | custom-call | tf_op jit(solution)/shard_map/pallas_call | solution.py:443

commit v5 on v4

--- a/solution.py
+++ b/solution.py
@@ -62,12 +62,25 @@
     def below(value, limit):
         return lax.bitwise_and(value, jnp.int32(limit - 1))
 
+    def hops(step, size):
+        return min(step, size - step)
+
+    ring = sorted(range(1, nz), key=lambda step: -hops(step, nz))
+    rows_y = np_ // 4
+    steps = sorted(
+        [(a, b, c) for a in range(4) for b in range(rows_y) for c in range(2)][1:],
+        key=lambda step: -(hops(step[0], 4) + hops(step[1], rows_y)))
+    my_x = 2 * lax.div(p, 2 * rows_y) + r
+    my_y = below(lax.div(p, 2), rows_y)
+    my_core = below(p, 2)
+
     def z_peer(k):
-        far = (k + 1) // 2
-        return below(z + (far if k % 2 else nz - far), nz)
+        return below(z + ring[k - 1], nz)
 
     def plane_peer(k):
-        return below(q + k, nq)
+        a, b, c = steps[k - 1]
+        to_x, to_y, to_core = below(my_x + a, 4), below(my_y + b, rows_y), below(my_core + c, 2)
+        return below(to_x, 2) * np_ + (lax.div(to_x, 2) * rows_y + to_y) * 2 + to_core
 
     def plane_device(other):
         return (z * np_ + below(other, np_), lax.div(other, np_))

time: 71.8 us -> 69.5 us (0.968)
  Pallas kernels: 71.1 us -> 68.7 us
    pallas_call x1, Pallas kernels: 69.2 us -> 66.8 us  [body(): pl.pallas_call(functools.partial(kernel, nz, np_, share, cols, pad, tall)...]
where the time goes in v5:
time: 69.5 us; the launch traced here: 69.4 us
  Pallas kernels  68.7 us (99%)
    pallas_call x1, Pallas kernels, body(): pl.pallas_call(functools.partial(kernel, nz, np_, share, cols, pad, tall)...  66.8 us
    pallas_call x1, Pallas kernels, body(): pl.pallas_call(write_out, out_shape=[jax.ShapeDtypeStruct(a.shape, a.dtyp...  1.95 us

profile of v5, /device:TPU:1, one launch (start us, length us, event | category | flops | bytes accessed | tf_op | source)
XLA Modules:
  0.0 69.4 jit_solution(1875190559433985683)
XLA Ops:
  0.6 66.8 %shard_map.76 = (bf16[256,1280]{1,0:T(8,128)(2,1)S(1)}, bf16[1280,1280]{1,0:T(8,128)(2,1)S(1)}, f32[10,128]{1,0:T(8,128)S(1)}) custom-call(bf16[256,1280]{1,0:T(8,128)(2,1)} %bitcast.8, bf16[1280,128]{1,0:T(8,128)(2,1)} %rt_hbm.1, bf16[1280,1280]{1,0:T(8,128)(2,1)} %bitcast.6, bf16[1280,1280]{1,0:T(8,128)(2,1)} %bitcast.7, bf16[256,1280]{1,0:T(8,128)(2,1)} %bitcast.9), custom_call_target="tpu_custom_call" | custom-call | tf_op jit(solution)/shard_map/pallas_call | solution.py:429
  67.4 1.9 %shard_map.77 = (bf16[256,1280]{1,0:T(8,128)(2,1)}, bf16[1280,1280]{1,0:T(8,128)(2,1)}, f32[10,128]{1,0:T(8,128)}) custom-call(bf16[256,1280]{1,0:T(8,128)(2,1)S(1)} %get-tuple-element.9.gt, bf16[1280,1280]{1,0:T(8,128)(2,1)S(1)} %get-tuple-element.10.gw, f32[10,128]{1,0:T(8,128)S(1)} %get-tuple-element.11.gr), custom_call_target="tpu_custom_call" | custom-call | tf_op jit(solution)/shard_map/pallas_call | solution.py:456

commit v6 on v5

--- a/solution.py
+++ b/solution.py
@@ -354,27 +354,22 @@
     mine = lax.div(z, upper)
 
     def hand_over(t):
-        level, other = lax.div(t, 2), lax.rem(t, 2)
+        level, other = t // 2, t % 2
         to = r * upper + level
         copy = pltpu.make_async_remote_copy(
             src_ref=rpart.at[level], dst_ref=rfin.at[z], send_sem=rf_s.at[t],
             recv_sem=rf_r.at[z], device_id=(to * np_ + p, other), device_id_type=MESH)
         return copy, (to != z) | (other != r)
 
-    @pl.loop(0, nz)
-    def _(t):
+    for t in range(nz):
         copy, away = hand_over(t)
-
-        @pl.when(away)
-        def _():
-            copy.start()
-
-        @pl.when(jnp.logical_not(away))
-        def _():
-            rfin[z] = rpart[lax.div(t, 2)]
-
-    @pl.loop(0, nz)
-    def _(k):
+        pl.when(away)(copy.start)
+
+    @pl.when(mine == r)
+    def _():
+        rfin[z] = rpart[below(z, upper)]
+
+    for k in range(nz):
         @pl.when((k != z) | (mine != r))
         def _():
             pltpu.make_async_remote_copy(
@@ -385,13 +380,9 @@
     gr[...] = jnp.sum(rfin[...].astype(F32), axis=0)[:share]
     all_of(rsend, nq - 1, rp_s, rp_r).wait_send()
 
-    @pl.loop(0, nz)
-    def _(t):
+    for t in range(nz):
         copy, away = hand_over(t)
-
-        @pl.when(away)
-        def _():
-            copy.wait_send()
+        pl.when(away)(copy.wait_send)
 
 
 def write_out(gt, gw, gr, gt_hbm, gw_hbm, gr_hbm, sem):

time: 69.5 us -> 69.4 us (level)
  no operation moved by 1% of the time
where the time goes in v6:
time: 69.4 us; the launch traced here: 69.3 us
  Pallas kernels  68.7 us (99%)
    pallas_call x1, Pallas kernels, body(): pl.pallas_call(functools.partial(kernel, nz, np_, share, cols, pad, tall)...  66.7 us
    pallas_call x1, Pallas kernels, body(): pl.pallas_call(write_out, out_shape=[jax.ShapeDtypeStruct(a.shape, a.dtyp...  1.95 us

profile of v6, /device:TPU:1, one launch (start us, length us, event | category | flops | bytes accessed | tf_op | source)
XLA Modules:
  0.0 69.3 jit_solution(16882449579756742764)
XLA Ops:
  0.6 66.7 %shard_map.76 = (bf16[256,1280]{1,0:T(8,128)(2,1)S(1)}, bf16[1280,1280]{1,0:T(8,128)(2,1)S(1)}, f32[10,128]{1,0:T(8,128)S(1)}) custom-call(bf16[256,1280]{1,0:T(8,128)(2,1)} %bitcast.8, bf16[1280,128]{1,0:T(8,128)(2,1)} %rt_hbm.1, bf16[1280,1280]{1,0:T(8,128)(2,1)} %bitcast.6, bf16[1280,1280]{1,0:T(8,128)(2,1)} %bitcast.7, bf16[256,1280]{1,0:T(8,128)(2,1)} %bitcast.9), custom_call_target="tpu_custom_call" | custom-call | tf_op jit(solution)/shard_map/pallas_call | solution.py:420
  67.4 1.9 %shard_map.77 = (bf16[256,1280]{1,0:T(8,128)(2,1)}, bf16[1280,1280]{1,0:T(8,128)(2,1)}, f32[10,128]{1,0:T(8,128)}) custom-call(bf16[256,1280]{1,0:T(8,128)(2,1)S(1)} %get-tuple-element.9.gt, bf16[1280,1280]{1,0:T(8,128)(2,1)S(1)} %get-tuple-element.10.gw, f32[10,128]{1,0:T(8,128)S(1)} %get-tuple-element.11.gr), custom_call_target="tpu_custom_call" | custom-call | tf_op jit(solution)/shard_map/pallas_call | solution.py:447
